TPU v7x, 128 devices: a whole 4x4x4 slice. The times are simulated.
128 devices in a mesh: tm: 32 (over y, x, core), stream: 4 (over z).
Axes of the slice: x: 4, y: 4, z: 4, core: 2. Of those that a mesh axis runs over, the one named last changes fastest.
Arguments:
- raw: bfloat16 [4, 6, 524288], P('stream', None, 'tm'), may hold values from -6 to 6
- starts: int32 [4, 131072], P('stream', 'tm'), may hold values from 0 to 1, as said below
- neg_owner: int32 [4, 1024, 4], P('stream', 'tm'), may hold values from 0 to 127, all different within a row; in each aligned block of 32 rows (0 to 31, 32 to 63, ..., all dimensions but the last counted through in order) at most 2 rows name the same one
- neg_block: int32 [4, 1024, 4], P('stream', 'tm'), may hold values from 0 to 31
- enc_weight: bfloat16 [24, 256], replicated, may hold values from -1.25 to 1.25
- tcn_weight: bfloat16 [4, 2, 256, 256], replicated, may hold values from -0.25 to 0.25
- pred_weight: bfloat16 [256, 256], replicated, may hold values from -0.375 to 0.375
Outputs:
- grad_latent: float32 [4, 131072, 256], P('stream', 'tm')
Inputs may be any that keep to these rules, and one draw needn't show every extreme that they name: `starts`: row 0 of every stream is 1. `neg_owner`: the owner is the flat device index tm * 4 + stream; each row names 4 different owners; within the 32 rows of one device no owner is named more than 2 times, a bound that some block reaches.
All inputs are finite; a program needn't handle non-finite values.
Results may differ from a plain program's by a relative error of at most 0.011.
Values may be sent and summed in bfloat16 or wider, within the bound.
No kernel may reach another device: no remote copies, remote signals or barrier semaphores. Data moves between devices by JAX's collectives and lax.ppermute only.
A program may use at most 192 MiB of HBM per device.

v0:
```python
import jax
import jax.numpy as jnp
from jax import lax
from jax.sharding import PartitionSpec as P

STRIDE = 4
LAYERS = 4
AHEAD = 4
BLOCK = 128
NEG = 4


score_scale = 10.0
epsilon = 1e-06


def shifted(block, axis, distance):
    devices = range(lax.axis_size(axis))
    route = [(i - distance, i) for i in devices if i - distance in devices]
    return lax.ppermute(block, axis, route)


def encode(raw_rows, enc_weight):
    channels, samples = raw_rows.shape
    patches = raw_rows.reshape(channels, samples // STRIDE, STRIDE).transpose(1, 2, 0)
    patches = patches.reshape(samples // STRIDE, STRIDE * channels)
    return jax.nn.silu(jnp.dot(patches, enc_weight, preferred_element_type=jnp.float32)).astype(
        jnp.bfloat16
    )


def shift_down(values, spacing):
    filler = jnp.zeros((spacing,) + values.shape[1:], values.dtype)
    return jnp.concatenate([filler, values[:-spacing]], axis=0)


def shift_up(values, spacing):
    filler = jnp.zeros((spacing,) + values.shape[1:], values.dtype)
    return jnp.concatenate([values[spacing:], filler], axis=0)


def build_masks(start_rows):
    running = jnp.cumsum(start_rows, dtype=jnp.int32)
    tap_gates = []
    for layer_index in range(LAYERS):
        spacing = 2**layer_index
        tap_gates.append(
            jnp.where(running - shift_down(running, spacing) == 0, 1.0, 0.0).astype(jnp.float32)
        )
    return tap_gates


def context_forward(hidden, tap_gates, tcn_weight):
    preacts = []
    for layer_index in range(LAYERS):
        spacing = 2**layer_index
        current = jnp.dot(hidden, tcn_weight[layer_index, 0], preferred_element_type=jnp.float32)
        earlier = jnp.dot(hidden, tcn_weight[layer_index, 1], preferred_element_type=jnp.float32)
        preact = current + shift_down(earlier, spacing) * tap_gates[layer_index][:, None]
        hidden = (hidden.astype(jnp.float32) + jax.nn.silu(preact)).astype(jnp.bfloat16)
        preacts.append(preact)
    return (hidden, preacts)


def context_backward(cotangent, preacts, tap_gates, tcn_weight):
    for layer_index in reversed(range(LAYERS)):
        spacing = 2**layer_index
        preact = preacts[layer_index]
        sigmoid_value = jax.nn.sigmoid(preact)
        gated_back = (cotangent * sigmoid_value * (1.0 + preact * (1.0 - sigmoid_value))).astype(
            jnp.bfloat16
        )
        current = jnp.dot(
            gated_back, tcn_weight[layer_index, 0].T, preferred_element_type=jnp.float32
        )
        earlier = jnp.dot(
            gated_back, tcn_weight[layer_index, 1].T, preferred_element_type=jnp.float32
        )
        earlier = earlier * tap_gates[layer_index][:, None]
        cotangent = cotangent + current + shift_up(earlier, spacing)
    return cotangent


def predict(context_rows, pred_weight):
    raw_pred = jnp.dot(context_rows, pred_weight, preferred_element_type=jnp.float32)
    pred_scale = lax.rsqrt(jnp.sum(raw_pred * raw_pred, axis=-1) + epsilon)
    pred_unit = raw_pred * pred_scale[:, None]
    return (pred_scale, pred_unit, pred_unit.astype(jnp.bfloat16))


def predict_back(query_grad, pred_scale, pred_unit, pred_weight):
    along = jnp.sum(pred_unit * query_grad, axis=-1, keepdims=True)
    pred_grad = (pred_scale[:, None] * (query_grad - along * pred_unit)).astype(jnp.bfloat16)
    return jnp.dot(pred_grad, pred_weight.T, preferred_element_type=jnp.float32)


def score_group(queries, targets, usable, negatives):
    target_f = targets.astype(jnp.float32)
    query_f = queries.astype(jnp.float32)
    target_scale = lax.rsqrt(jnp.sum(target_f * target_f, axis=-1) + epsilon)
    neg_f = negatives.astype(jnp.float32)
    neg_scale = lax.rsqrt(jnp.sum(neg_f * neg_f, axis=-1) + epsilon)
    positive = score_scale * jnp.sum(query_f * target_f, axis=-1) * target_scale
    scores = (
        score_scale
        * jnp.einsum("gid,gkd->gik", queries, negatives, preferred_element_type=jnp.float32)
        * neg_scale[:, None, :]
    )
    exp_pos = jnp.exp(positive)
    exp_neg = jnp.exp(scores)
    partition = exp_pos + jnp.sum(exp_neg, axis=-1)
    d_pos = usable * (exp_pos / partition - 1.0)
    d_score = usable[:, :, None] * exp_neg / partition[:, :, None]
    weighted = (d_score * neg_scale[:, None, :]).astype(jnp.bfloat16)
    query_grad = score_scale * (
        jnp.einsum("gik,gkd->gid", weighted, negatives, preferred_element_type=jnp.float32)
        + (d_pos * target_scale)[:, :, None] * target_f
    )
    target_grad = (score_scale * d_pos * target_scale)[:, :, None] * query_f - (
        d_pos * positive * target_scale * target_scale
    )[:, :, None] * target_f
    direct = score_scale * jnp.einsum(
        "gik,gid->gkd", weighted, queries, preferred_element_type=jnp.float32
    )
    spread = jnp.sum(d_score * scores, axis=1)
    negative_grad = (direct - (spread * neg_scale * neg_scale)[:, :, None] * neg_f).astype(
        jnp.bfloat16
    )
    return (query_grad, target_grad, negative_grad)


def body(raw, starts, neg_owner, neg_block, enc_weight, tcn_weight, pred_weight):
    latents = encode(raw[0], enc_weight)
    lat_rows, channels = latents.shape
    rim_rows = 2**LAYERS - 1 + AHEAD
    rim_latents, rim_starts = shifted((latents[-rim_rows:], starts[0, -rim_rows:]), "tm", 1)
    ext_latents = jnp.concatenate([rim_latents, latents], axis=0)
    ext_starts = jnp.concatenate([rim_starts, starts[0]], axis=0)
    tap_gates = build_masks(ext_starts)
    context, preacts = context_forward(ext_latents, tap_gates, tcn_weight)
    lead = rim_rows - AHEAD
    pred_scale, pred_unit, queries = predict(context[lead : lead + lat_rows], pred_weight)
    running = jnp.cumsum(ext_starts, dtype=jnp.int32)
    usable = jnp.where(running[rim_rows:] - running[lead : lead + lat_rows] == 0, 1.0, 0.0).astype(
        jnp.float32
    )
    blocks = lat_rows // BLOCK
    owners_count = lax.axis_size("tm") * lax.axis_size("stream")
    capacity = max(2, 2 * blocks * NEG // owners_count)
    owner_list = neg_owner[0].reshape(-1)
    block_list = neg_block[0].reshape(-1)
    owner_hits = (owner_list[:, None] == jnp.arange(owners_count, dtype=jnp.int32)[None, :]).astype(
        jnp.int32
    )
    slot_rank = jnp.sum(
        (jnp.cumsum(owner_hits, axis=0, dtype=jnp.int32) - owner_hits) * owner_hits, axis=1
    )
    slot_index = owner_list * capacity + slot_rank
    wanted = jnp.zeros((owners_count * capacity,), jnp.int32).at[slot_index].set(block_list)
    requested = lax.all_to_all(
        wanted.reshape(owners_count, capacity),
        ("tm", "stream"),
        split_axis=0,
        concat_axis=0,
        tiled=True,
    )
    answer = latents.reshape(blocks, BLOCK, channels)[requested]
    fetched = lax.all_to_all(answer, ("tm", "stream"), split_axis=0, concat_axis=0, tiled=True)
    fetched_flat = fetched.reshape(owners_count * capacity, BLOCK, channels)
    group_blocks = 4
    groups = blocks // group_blocks

    def score_step(unused_carry, inputs):
        group_queries, group_targets, group_usable, group_slots = inputs
        negatives = fetched_flat[group_slots].reshape(group_blocks, NEG * BLOCK, channels)
        return (unused_carry, score_group(group_queries, group_targets, group_usable, negatives))

    unused_carry, outputs = lax.scan(
        score_step,
        jnp.zeros((), jnp.float32),
        (
            queries.reshape(groups, group_blocks, BLOCK, channels),
            latents.reshape(groups, group_blocks, BLOCK, channels),
            usable.reshape(groups, group_blocks, BLOCK),
            slot_index.reshape(groups, group_blocks, NEG),
        ),
    )
    query_grad, target_grad, negative_grad = outputs
    outgoing = jnp.zeros((owners_count * capacity, BLOCK, channels), jnp.bfloat16)
    outgoing = outgoing.at[slot_index].set(negative_grad.reshape(blocks * NEG, BLOCK, channels))
    returned = lax.all_to_all(
        outgoing.reshape(owners_count, capacity, BLOCK, channels),
        ("tm", "stream"),
        split_axis=0,
        concat_axis=0,
        tiled=True,
    )
    block_hits = (
        requested.reshape(-1)[:, None] == jnp.arange(blocks, dtype=jnp.int32)[None, :]
    ).astype(jnp.bfloat16)
    neg_total = jnp.einsum(
        "sb,sf->bf",
        block_hits,
        returned.reshape(owners_count * capacity, BLOCK * channels),
        preferred_element_type=jnp.float32,
    )
    context_rows = predict_back(
        query_grad.reshape(lat_rows, channels), pred_scale, pred_unit, pred_weight
    )
    context_grad = jnp.concatenate(
        [
            jnp.zeros((lead, channels), jnp.float32),
            context_rows,
            jnp.zeros((AHEAD, channels), jnp.float32),
        ],
        axis=0,
    )
    ext_grad = context_backward(context_grad, preacts, tap_gates, tcn_weight)
    borrowed = shifted(ext_grad[:rim_rows], "tm", -1)
    gradient = (
        ext_grad[rim_rows:]
        + target_grad.reshape(lat_rows, channels)
        + neg_total.reshape(lat_rows, channels)
    )
    gradient = gradient + jnp.concatenate(
        [jnp.zeros((lat_rows - rim_rows, channels), jnp.float32), borrowed], axis=0
    )
    return gradient[None]


def solution(mesh):
    placed = (
        P("stream", None, "tm"),
        P("stream", "tm"),
        P("stream", "tm", None),
        P("stream", "tm", None),
        P(),
        P(),
        P(),
    )
    return jax.shard_map(
        body, mesh=mesh, in_specs=placed, out_specs=P("stream", "tm", None), check_vma=False
    )
```

profile of v0, /device:TPU:10, one launch (start us, length us, event | category | flops | bytes accessed | tf_op | source)
XLA Modules:
  0.0 723.3 jit_solution(10734674801912981676)
XLA Ops:
  4.9 10.4 %all-to-all-start = ((s32[128,1,2]{2,1,0:T(1,128)}), s32[128,1,2]{2,1,0:T(1,128)S(1)}, u32[]{:S(2)}, u32[]{:S(2)}) async-start(s32[128,1,2]{2,1,0:T(1,128)} %bitcast.25), calls=%async_computation | async-start | bytes 131072 | tf_op jit(solution)/shard_map/all_to_all | solution.py:160
  15.3 17.4 %reshape_squeeze.7 = bf16[6,4096,4]{2,1,0:T(8,128)(2,1)} reshape(bf16[1,6,16384]{2,1,0:T(8,128)(2,1)} %param.9) | data formatting | bytes 393216 | tf_op jit(solution)/shard_map/reshape;squeeze | solution.py:25
  32.7 5.8 copy.22
  40.2 9.4 %gather_fusion.1 = bf16[256,128,256]{2,1,0:T(8,128)(2,1)} fusion(bf16[32,128,256]{2,1,0:T(8,128)(2,1)S(1)} %bitcast.188, s32[1024]{0:T(1024)S(1)} %pad_clamp_fusion.1), kind=kCustom, calls=%fused_computation.1 | custom fusion | bytes 33555456 | tf_op jit(solution)/shard_map/gather | solution.py:167
  49.5 10.4 %all-to-all-start.1 = ((bf16[128,2,128,256]{3,2,1,0:T(8,128)(2,1)}), bf16[128,2,128,256]{3,2,1,0:T(8,128)(2,1)}, u32[]{:S(2)}, u32[]{:S(2)}) async-start(bf16[128,2,128,256]{3,2,1,0:T(8,128)(2,1)} %bitcast.191), calls=%async_computation.1 | async-start | bytes 33554432 | tf_op jit(solution)/shard_map/all_to_all | solution.py:168
  62.0 3.3 collective-permute-start
  65.8 199.9 %collective-permute-done.1 = s32[19]{0:T(128)S(1)} collective-permute-done((s32[19]{0:T(128)S(1)}, s32[19]{0:T(128)S(1)}, u32[]{:S(2)}, u32[]{:S(2)}) %collective-permute-start.1) | collective-permute-done | bytes 108 | tf_op jit(solution)/shard_map/ppermute | solution.py:20
  267.3 4.9 add_convert_fusion.2
  272.9 4.4 add_convert_fusion.1
  278.1 4.5 add_convert_fusion
  290.5 128.9 %while.16 = (s32[]{:T(128)}, f32[8,4,128,256]{3,2,1,0:T(8,128)}, f32[8,4,128,256]{3,2,1,0:T(8,128)}, bf16[8,4,512,256]{3,2,1,0:T(8,128)(2,1)}, f32[8,4,128]{2,1,...) while((s32[]{:T(128)}, f32[8,4,128,256]{3,2,1,0:T(8,128)}, ...), condition=%wide.region_12.13_spmd, body=%wide.region_6.12_spmd.sunk | while | flops 412495424 | bytes 14597893 | solution.py:178
  291.9 6.4 gather_fusion
  308.0 6.4 gather_fusion
  324.1 6.4 gather_fusion
  340.2 6.4 gather_fusion
  356.3 6.4 gather_fusion
  372.4 6.4 gather_fusion
  388.5 6.4 gather_fusion
  404.6 6.4 gather_fusion
  419.4 6.0 broadcast_in_dim.85
  425.3 23.5 %scatter_fusion = bf16[256,128,256]{2,1,0:T(8,128)(2,1)} fusion(bf16[256,128,256]{2,1,0:T(8,128)(2,1)} %broadcast_in_dim.85, s32[128]{0:T(128)S(1)} %fusion.91, bf16[128,128,256]{2,1,0:T(8,128)(2,1)} %bitcast.197), kind=kCustom, calls=%fused_computation.3 | custom fusion | bytes 25166336 | tf_op jit(solution)/shard_map/scatter | solution.py:190
  448.9 17.8 %all-to-all-start.2 = ((bf16[128,2,128,256]{3,2,1,0:T(8,128)(2,1)}), bf16[128,2,128,256]{3,2,1,0:T(8,128)(2,1)}, u32[]{:S(2)}, u32[]{:S(2)}) async-start(bf16[128,2,128,256]{3,2,1,0:T(8,128)(2,1)} %bitcast.190), calls=%async_computation.2 | async-start | bytes 33554432 | tf_op jit(solution)/shard_map/all_to_all | solution.py:191
  468.4 4.3 fusion.28
  479.4 12.8 %concatenate.58 = f32[4115,256]{1,0:T(8,128)} concatenate(f32[15,256]{1,0:T(8,128)S(1)} %broadcast_in_dim.78, f32[4096,256]{1,0:T(8,128)} %fusion.96, f32[4,256]{1,0:T(4,128)S(1)} %broadcast.286), dimensions={0} | concatenate | bytes 8427520 | tf_op jit(solution)/shard_map/concatenate | solution.py:210
  492.2 5.0 multiply_convert_fusion.6
  499.9 3.7 multiply_convert_fusion.5
  506.2 4.0 multiply_convert_fusion.4
  523.1 166.5 %all-to-all-done.2 = bf16[128,2,128,256]{3,2,1,0:T(8,128)(2,1)} async-done(((bf16[128,2,128,256]{3,2,1,0:T(8,128)(2,1)}), bf16[128,2,128,256]{3,2,1,0:T(8,128)(2,1)}, u32[]{:S(2)}, u32[]{:S(2)}) %all-to-all-start.2) | async-done | bytes 16777248 | tf_op jit(solution)/shard_map/all_to_all | solution.py:191
  689.6 15.8 %copy.31 = bf16[32,8,128,256]{3,1,2,0:T(8,128)(2,1)S(1)} copy(bf16[32,8,128,256]{3,2,1,0:T(8,128)(2,1)} %bitcast.40) | data formatting | bytes 33554432
  705.4 5.0 fusion.65
  710.5 4.9 reshape.289
  715.4 7.5 %fusion.25 = f32[1,4096,256]{2,1,0:T(8,128)} fusion(f32[4096,256]{1,0:T(8,128)} %reshape.289, f32[4115,256]{1,0:T(8,128)} %copy-done.3, f32[8,4,128,256]{3,2,1,0:T(8,128)} %get-tuple-element.121, f32[19,256]{1,0:T(8,128)S(1)} %collective-permute-done.2), kind=kLoop, calls=%fused_computation.76 | loop fusion | flops 3145728 | bytes 16796672 | tf_op jit(solution)/shard_map/broadcast_in_dim | solution.py:228
  (256 shorter events, 123.4 us)
Async XLA Ops:
  0.0 284.8 %copy-start = (bf16[256,256]{1,0:T(8,128)(2,1)S(1)}, bf16[256,256]{1,0:T(8,128)(2,1)}, u32[]{:S(2)}) copy-start(bf16[256,256]{1,0:T(8,128)(2,1)} %param.15) | copy-start | bytes 393220
  4.9 35.1 %all-to-all-start = ((s32[128,1,2]{2,1,0:T(1,128)}), s32[128,1,2]{2,1,0:T(1,128)S(1)}, u32[]{:S(2)}, u32[]{:S(2)}) async-start(s32[128,1,2]{2,1,0:T(1,128)} %bitcast.25), calls=%async_computation | async-start | bytes 131072 | tf_op jit(solution)/shard_map/all_to_all | solution.py:160
  32.7 5.9 copy-start.9
  49.5 10.4 %copy-start.8 = (s32[1,4096]{1,0:T(1,128)S(1)}, s32[1,4096]{1,0:T(1,128)}, u32[]{:S(2)}) copy-start(s32[1,4096]{1,0:T(1,128)} %param.10) | copy-start | bytes 49156
  49.5 217.1 %copy-start.6 = (bf16[4,2,256,256]{3,2,1,0:T(8,128)(2,1)S(1)}, bf16[4,2,256,256]{3,2,1,0:T(8,128)(2,1)}, u32[]{:S(2)}) copy-start(bf16[4,2,256,256]{3,2,1,0:T(8,128)(2,1)} %param.14) | copy-start | bytes 3145732
  49.5 241.0 %all-to-all-start.1 = ((bf16[128,2,128,256]{3,2,1,0:T(8,128)(2,1)}), bf16[128,2,128,256]{3,2,1,0:T(8,128)(2,1)}, u32[]{:S(2)}, u32[]{:S(2)}) async-start(bf16[128,2,128,256]{3,2,1,0:T(8,128)(2,1)} %bitcast.191), calls=%async_computation.1 | async-start | bytes 33554432 | tf_op jit(solution)/shard_map/all_to_all | solution.py:168
  60.0 205.7 %collective-permute-start.1 = (s32[19]{0:T(128)S(1)}, s32[19]{0:T(128)S(1)}, u32[]{:S(2)}, u32[]{:S(2)}) collective-permute-start(s32[19]{0:T(128)S(1)} %slice_bitcast_fusion), channel_id=1, source_target_pairs={{0,4},{4,8},{8,12},{12,16},{16,20},{20,24},{24,28},{28,32},{32,36}... | collective-permute-start | bytes 236 | tf_op jit(solution)/shard_map/ppermute | solution.py:20
  62.0 204.5 %collective-permute-start = (bf16[19,256]{1,0:T(8,128)(2,1)S(1)}, bf16[19,256]{1,0:T(8,128)(2,1)S(1)}, u32[]{:S(2)}, u32[]{:S(2)}) collective-permute-start(bf16[19,256]{1,0:T(8,128)(2,1)S(1)} %slice.143), channel_id=1, source_target_pairs={{0,4},{4,8},{8,12},{12,16},{16,20},{20,24},{24,28},{28,32},{32,36}... | collective-permute-start | bytes 29192 | tf_op jit(solution)/shard_map/ppermute | solution.py:20
  284.8 2.1 copy-start.5
  286.9 1.9 copy-start.1
  448.9 240.8 %all-to-all-start.2 = ((bf16[128,2,128,256]{3,2,1,0:T(8,128)(2,1)}), bf16[128,2,128,256]{3,2,1,0:T(8,128)(2,1)}, u32[]{:S(2)}, u32[]{:S(2)}) async-start(bf16[128,2,128,256]{3,2,1,0:T(8,128)(2,1)} %bitcast.190), calls=%async_computation.2 | async-start | bytes 33554432 | tf_op jit(solution)/shard_map/all_to_all | solution.py:191
  468.4 4.7 copy-start.2
  468.4 5.9 copy-start.4
  492.2 5.0 copy-start.7
  492.2 7.6 %slice-start = ((s8[4218880]{0:T(1024)(128)(4,1)}), s8[24576]{0:T(1024)(128)(4,1)S(1)}, s32[]{:S(2)}) async-start(s8[4218880]{0:T(1024)(128)(4,1)} %bitcast.195), calls=%async_computation.3 | async-start | bytes 49152
  492.2 7.6 %slice-start.6 = ((s8[4218880]{0:T(1024)(128)(4,1)}), s8[4194304]{0:T(1024)(128)(4,1)S(1)}, s32[]{:S(2)}) async-start(s8[4218880]{0:T(1024)(128)(4,1)} %bitcast.209), calls=%async_computation.9 | async-start | bytes 8388608
  497.2 2.6 slice-start.1
  497.2 2.6 slice-start.7
  498.0 8.2 %slice-start.4 = ((s8[4218880]{0:T(1024)(128)(4,1)}), s8[4194304]{0:T(1024)(128)(4,1)S(1)}, s32[]{:S(2)}) async-start(s8[4218880]{0:T(1024)(128)(4,1)} %bitcast.207), calls=%async_computation.7 | async-start | bytes 8388608
  499.8 6.3 slice-start.5
  504.3 8.6 %slice-start.2 = ((s8[4218880]{0:T(1024)(128)(4,1)}), s8[4194304]{0:T(1024)(128)(4,1)S(1)}, s32[]{:S(2)}) async-start(s8[4218880]{0:T(1024)(128)(4,1)} %bitcast.205), calls=%async_computation.5 | async-start | bytes 8388608
  506.2 6.8 slice-start.3
  518.8 2.1 copy-start.3
  520.9 194.5 %collective-permute-start.2 = (f32[19,256]{1,0:T(8,128)S(1)}, f32[19,256]{1,0:T(8,128)S(1)}, u32[]{:S(2)}, u32[]{:S(2)}) collective-permute-start(f32[19,256]{1,0:T(8,128)S(1)} %slice.170), channel_id=1, source_target_pairs={{4,0},{8,4},{12,8},{16,12},{20,16},{24,20},{28,24},{32,28},{36,32}... | collective-permute-start | bytes 58376 | tf_op jit(solution)/shard_map/ppermute | solution.py:20
where the time goes:
time: 735 us; the launch traced here: 723 us
  waiting for transfers between devices  366 us (50%)
  local copies, waits for them, and re-layouts  159 us (22%)
  matrix products  88.2 us (12%)
  other arithmetic  61.8 us (8%)
  starting transfers between devices  46.1 us (6%)
    ppermute x3, waiting for transfers between devices, shifted(): return lax.ppermute(block, axis, route)  200 us
    all_to_all x1, waiting for transfers between devices, body(): lax.all_to_all(outgoing.reshape(owners_count, capacity, BLOCK, channels),...  167 us
    gather x8, local copies, waits for them, and re-layouts, score_step(): fetched_flat[group_slots].reshape(group_blocks, NEG * BLOCK, channels)  51.1 us
    scatter x1, local copies, waits for them, and re-layouts, body(): outgoing.at[slot_index]  23.5 us
    unnamed x39, local copies, waits for them, and re-layouts  22.9 us
    dot_general x8, matrix products, score_group(): jnp.einsum('gik,gid->gkd', weighted, queries, preferred_element_type=jnp....  22.6 us
    all_to_all x1, starting transfers between devices, body(): lax.all_to_all(outgoing.reshape(owners_count, capacity, BLOCK, channels),...  17.8 us
    another operation x1, local copies, waits for them, and re-layouts, encode(): raw_rows.reshape(channels, samples // STRIDE, STRIDE).transpose(1, 2, 0)  17.4 us
  transfers between devices with their start and end apart: 6, of which 2 were waited for; matrix products, arithmetic and copies ran while one was open for 17% of the time, Pallas kernels for 0%

commit v1 on v0

v1 whole, which is shorter than its diff:
```python
import jax
import jax.numpy as jnp
from jax import lax
from jax.experimental import pallas as pl
from jax.experimental.pallas import tpu as pltpu
from jax.sharding import PartitionSpec as P

BLOCK = 128
NEG = 4
HALO = 32
AHEAD = 4
CAP = 2
LAYERS = 4
PACK = 32
TOGETHER = 8
SEGMENT = 512
SCALE = 10.0
EPSILON = 1e-06
BF = jnp.bfloat16
F32 = jnp.float32
MIB = 1 << 20


def dot(a, b):
    return jnp.dot(a, b, preferred_element_type=F32)


def dot_nt(a, b):
    return lax.dot_general(a, b, (((1,), (1,)), ((), ())), preferred_element_type=F32)


def row_sum(x):
    return jnp.sum(x, axis=-1, keepdims=True)


def silu_of_half(half):
    return half + half * jnp.tanh(half)


def prep_kernel(owner_ref, block_ref, raw_ref, starts_ref, rim_ref, enc_ref,
                pack_ref, push_ref, slot_ref, bd_ref, lines, packs, seen):
    blocks = pack_ref.shape[0]
    lines[...] = jnp.zeros_like(lines)
    for b in range(blocks):
        lines[b, 0:6, :] = raw_ref[:, b * 512:(b + 1) * 512].astype(F32)
    row = lax.broadcasted_iota(jnp.int32, (512, 512), 0)
    col = lax.broadcasted_iota(jnp.int32, (512, 512), 1)
    perm = jnp.where(row == 4 * (col & 127) + (col >> 7), 1.0, 0.0).astype(BF)
    row = lax.broadcasted_iota(jnp.int32, (128, 128), 0)
    col = lax.broadcasted_iota(jnp.int32, (128, 128), 1)
    perm_halo = jnp.where(row == 4 * (col & 31) + (col >> 5), 1.0, 0.0).astype(BF)
    flat = lines[...].reshape(blocks * 8, 512).astype(BF)
    main = dot(flat, perm).reshape(blocks, 8, 512)
    halo = dot(flat[:, 384:512], perm_halo).reshape(blocks, 8, 128)
    rim = rim_ref[...]
    rim_halo = dot(rim, perm_halo)

    lane = lax.broadcasted_iota(jnp.int32, (blocks + 8, 128), 1)
    level_row = lax.broadcasted_iota(jnp.int32, (8, 128), 0)
    rim_f = rim.astype(F32)
    before = jnp.where(level_row == 7, pltpu.roll(rim_f, 1, 0), 0.0)
    started = jnp.concatenate([before, starts_ref[...].astype(F32)], axis=0)
    level = 1.0 - started
    for distance in (1, 2, 4):
        moved = pltpu.roll(started, distance, 1)
        started = jnp.maximum(
            started, jnp.where(lane < distance, pltpu.roll(moved, 1, 0), moved)
        )
        level = level + (1.0 - started)
    level_halo = jnp.where(lane < HALO, pltpu.roll(level, HALO, 1), 0.0)

    for k in range(4):
        packs[:, k * 6:(k + 1) * 6, :] = main[:, 0:6, k * 128:(k + 1) * 128]
    packs[0, 24:30, :] = rim_halo[0:6]
    packs[1:blocks, 24:30, :] = halo[0:blocks - 1, 0:6, :]
    for b in range(blocks):
        packs[b, 30:31, :] = level[8 + b:9 + b]
        packs[b, 31:32, :] = level_halo[7 + b:8 + b]
    pack_ref[...] = packs[...].astype(BF)

    at = lax.broadcasted_iota(jnp.int32, (PACK, 128), 0)
    lane = lax.broadcasted_iota(jnp.int32, (PACK, 128), 1)
    note = jnp.where((at == PACK - 1) & (lane >= 64), 1.0, 0.0)
    unused = (-note).astype(BF)

    def clear(i, carry):
        push_ref[i] = unused
        return carry

    lax.fori_loop(0, push_ref.shape[0], clear, 0)

    def forget(i, carry):
        seen[i] = 0
        return carry

    lax.fori_loop(0, seen.shape[0], forget, 0)

    def send(i, carry):
        owner = owner_ref[i]
        rank = seen[owner]
        seen[owner] = rank + 1
        slot = owner * CAP + rank
        slot_ref[i] = slot
        wanted = block_ref[i].astype(F32)
        push_ref[slot] = (packs[i // NEG] + note * wanted).astype(BF)
        return carry

    lax.fori_loop(0, blocks * NEG, send, 0)

    bd_ref[...] = jnp.zeros_like(bd_ref)
    half_enc = (enc_ref[...].astype(F32) * 0.5).astype(BF)
    for q in range(4):
        bd_ref[q * 32:q * 32 + 24, q * 256:(q + 1) * 256] = half_enc


def prep(owners, wanted, raw, starts, rim, enc_weight, owners_count):
    blocks = starts.shape[0]
    smem = pl.BlockSpec(memory_space=pltpu.SMEM)
    vmem = pl.BlockSpec(memory_space=pltpu.VMEM)
    return pl.pallas_call(
        prep_kernel,
        out_shape=(
            jax.ShapeDtypeStruct((blocks, PACK, 128), BF),
            jax.ShapeDtypeStruct((owners_count * CAP, PACK, 128), BF),
            jax.ShapeDtypeStruct((blocks * NEG,), jnp.int32),
            jax.ShapeDtypeStruct((128, 1024), BF),
        ),
        in_specs=[smem, smem, vmem, vmem, vmem, vmem],
        out_specs=(vmem, vmem, smem, vmem),
        scratch_shapes=[
            pltpu.VMEM((blocks, 8, 512), F32),
            pltpu.VMEM((blocks, PACK, 128), F32),
            pltpu.SMEM((owners_count,), jnp.int32),
        ],
        compiler_params=pltpu.CompilerParams(vmem_limit_bytes=32 * MIB),
        name="prep",
    )(owners, wanted, raw, starts, rim, enc_weight)


def turn(tiles):
    return jnp.transpose(jnp.concatenate(tiles, axis=0).astype(F32))


def encode_with_halo(turned, bd):
    lane = lax.broadcasted_iota(jnp.int32, (HALO, 128), 1) & 31
    halo = jnp.zeros((HALO, 128), F32)
    for k in range(4):
        moved = pltpu.roll(turned[k * 32:(k + 1) * 32], (6 * k - 24) % 128, 1)
        halo = jnp.where((lane >= 6 * k) & (lane < 6 * k + 6), moved, halo)
    rows = jnp.concatenate([turned, halo], axis=0).astype(BF)
    return silu_of_half(dot(rows, bd))


def layer_half(h, level, layer, w_ref):
    moved = pltpu.roll(h, 2**layer, 0)
    gated = jnp.where(level > layer, moved, 0.0)
    return dot(h.astype(BF), w_ref[layer, 0]) + dot(gated.astype(BF), w_ref[layer, 1])


def forward_kernel(pack_ref, bd_ref, w_ref, pred_ref, lat_ref, ctx_ref, slope_ref, level_ref,
                   rim_slope_ref, rim_level_ref, keyed_ref):
    first = pl.program_id(0) == 0
    turned = turn([pack_ref[q] for q in range(4)])
    encoded = encode_with_halo(turned, bd_ref[...])
    latent = jnp.concatenate(
        [encoded[128:160, 0:256]] + [encoded[0:128, q * 256:(q + 1) * 256] for q in range(4)],
        axis=0,
    ).astype(BF)
    columns = [turned[0:32, 31:32]] + [turned[:, q * 32 + 30:q * 32 + 31] for q in range(4)]
    level = jnp.broadcast_to(jnp.concatenate(columns, axis=0), (HALO + SEGMENT, 256))
    level_ref[...] = level[HALO:, 0:128]
    lat_ref[...] = latent[HALO:]
    h = latent.astype(F32)
    own = h[HALO:]
    key_scale = lax.rsqrt(row_sum(own * own) + EPSILON)
    keyed_ref[...] = dot_nt((own * key_scale).astype(BF), pred_ref[...]).astype(BF)
    slopes = []
    for layer in range(LAYERS):
        half = layer_half(h, level, layer, w_ref)
        tanh = jnp.tanh(half)
        slope = (0.5 * (1.0 + tanh)) * (1.0 + half * (1.0 - tanh))
        slope_ref[layer] = slope[HALO:].astype(BF)
        slopes.append(slope[:HALO].astype(BF))
        h = h + half + half * tanh
    ctx_ref[...] = h[HALO - AHEAD:HALO - AHEAD + SEGMENT].astype(BF)

    @pl.when(first)
    def _():
        rim_level_ref[...] = level[:HALO, 0:128]
        for layer in range(LAYERS):
            rim_slope_ref[layer] = slopes[layer]


def forward(pack, bd, half_weight, pred_weight):
    rows = pack.shape[0] * BLOCK
    steps = rows // SEGMENT
    whole = lambda *shape: pl.BlockSpec(shape, lambda i: (0,) * len(shape))
    rows_of = lambda width: pl.BlockSpec((SEGMENT, width), lambda i: (i, 0))
    return pl.pallas_call(
        forward_kernel,
        grid=(steps,),
        out_shape=(
            jax.ShapeDtypeStruct((rows, 256), BF),
            jax.ShapeDtypeStruct((rows, 256), BF),
            jax.ShapeDtypeStruct((LAYERS, rows, 256), BF),
            jax.ShapeDtypeStruct((rows, 128), F32),
            jax.ShapeDtypeStruct((LAYERS, HALO, 256), BF),
            jax.ShapeDtypeStruct((HALO, 128), F32),
            jax.ShapeDtypeStruct((rows, 256), BF),
        ),
        in_specs=[
            pl.BlockSpec((4, PACK, 128), lambda i: (i, 0, 0)),
            whole(128, 1024),
            whole(LAYERS, 2, 256, 256),
            whole(256, 256),
        ],
        out_specs=(
            rows_of(256),
            rows_of(256),
            pl.BlockSpec((LAYERS, SEGMENT, 256), lambda i: (0, i, 0)),
            rows_of(128),
            whole(LAYERS, HALO, 256),
            whole(HALO, 128),
            rows_of(256),
        ),
        compiler_params=pltpu.CompilerParams(vmem_limit_bytes=40 * MIB),
        cost_estimate=pl.CostEstimate(
            flops=rows * 2 * 65536 * 10, bytes_accessed=18 * MIB, transcendentals=rows * 256 * 5
        ),
        name="forward",
    )(pack, bd, half_weight, pred_weight)


def answer_kernel(wanted_ref, pack_ref, answer_ref, order_ref, count_ref):
    slots = wanted_ref.shape[0]

    def clear(i, carry):
        order_ref[i] = 0
        return carry

    lax.fori_loop(0, slots, clear, 0)

    def reply(i, count):
        wanted = wanted_ref[i]
        answer_ref[i] = pack_ref[jnp.maximum(wanted, 0)]
        order_ref[count] = i
        return count + jnp.where(wanted >= 0, 1, 0)

    count = lax.fori_loop(0, slots, reply, 0)
    count_ref[0] = count


def answer(wanted, pack):
    slots = wanted.shape[0]
    smem = pl.BlockSpec(memory_space=pltpu.SMEM)
    vmem = pl.BlockSpec(memory_space=pltpu.VMEM)
    return pl.pallas_call(
        answer_kernel,
        out_shape=(
            jax.ShapeDtypeStruct((slots, PACK, 128), BF),
            jax.ShapeDtypeStruct((slots,), jnp.int32),
            jax.ShapeDtypeStruct((1,), jnp.int32),
        ),
        in_specs=[smem, vmem],
        out_specs=(vmem, smem, smem),
        compiler_params=pltpu.CompilerParams(vmem_limit_bytes=16 * MIB),
        name="answer",
    )(wanted, pack)


def recompute_kernel(order_ref, count_ref, push_ref, bd_ref, w_ref, ctx_ref):
    base = pl.program_id(0) * TOGETHER

    @pl.when(base < count_ref[0])
    def _():
        bd = bd_ref[...]
        hidden, levels = [], []
        for part in range(TOGETHER // 4):
            turned = turn([push_ref[order_ref[base + part * 4 + q]] for q in range(4)])
            encoded = encode_with_halo(turned, bd)
            for q in range(4):
                hidden.append(encoded[128:160, q * 256:(q + 1) * 256])
                hidden.append(encoded[0:128, q * 256:(q + 1) * 256])
                levels.append(turned[0:32, q * 32 + 31:q * 32 + 32])
                levels.append(turned[:, q * 32 + 30:q * 32 + 31])
        h = jnp.concatenate(hidden, axis=0)
        level = jnp.broadcast_to(jnp.concatenate(levels, axis=0), h.shape)
        for layer in range(LAYERS):
            h = h + silu_of_half(layer_half(h, level, layer, w_ref))
        for j in range(TOGETHER):
            at = j * (HALO + BLOCK) + HALO - AHEAD
            ctx_ref[j] = h[at:at + BLOCK].astype(BF)


def last_step(count_ref):
    return jnp.maximum(count_ref[0] - 1, 0) // TOGETHER


def recompute(order, count, pushed, bd, half_weight):
    slots = pushed.shape[0]
    whole = lambda *shape: pl.BlockSpec(shape, lambda i, o, c: (0,) * len(shape))
    return pl.pallas_call(
        recompute_kernel,
        grid_spec=pltpu.PrefetchScalarGridSpec(
            num_scalar_prefetch=2,
            grid=(slots // TOGETHER,),
            in_specs=[whole(slots, PACK, 128), whole(128, 1024), whole(LAYERS, 2, 256, 256)],
            out_specs=pl.BlockSpec(
                (TOGETHER, BLOCK, 256), lambda i, o, c: (jnp.minimum(i, last_step(c)), 0, 0)
            ),
        ),
        out_shape=jax.ShapeDtypeStruct((slots, BLOCK, 256), BF),
        compiler_params=pltpu.CompilerParams(vmem_limit_bytes=48 * MIB),
        cost_estimate=pl.CostEstimate(
            flops=slots * 160 * 2 * 65536 * 10, bytes_accessed=20 * MIB,
            transcendentals=slots * 160 * 256 * 5,
        ),
        name="recompute",
    )(order, count, pushed, bd, half_weight)


def score_kernel(slot_ref, answer_ref, ctx_ref, lat_ref, level_ref, pred_ref, bd_ref,
                 pred_grad_ref, target_grad_ref, stats_ref):
    block = pl.program_id(0)
    raw_pred = dot(ctx_ref[...], pred_ref[...])
    pred_scale = lax.rsqrt(row_sum(raw_pred * raw_pred) + EPSILON)
    unit = raw_pred * pred_scale
    query = unit.astype(BF)
    query_f = query.astype(F32)

    turned = turn([answer_ref[slot_ref[block * NEG + j]] for j in range(NEG)])
    encoded = silu_of_half(dot(turned.astype(BF), bd_ref[...]))
    keys = []
    for j in range(NEG):
        negative = encoded[:, j * 256:(j + 1) * 256]
        key_scale = lax.rsqrt(row_sum(negative * negative) + EPSILON)
        keys.append((negative * key_scale).astype(BF))
    keys = jnp.concatenate(keys, axis=0)

    latent = lat_ref[...].astype(F32)
    usable = jnp.where(level_ref[:, 0:1] > 2.0, 1.0, 0.0)
    own_scale = lax.rsqrt(row_sum(latent * latent) + EPSILON)
    positive = SCALE * row_sum(query_f * latent) * own_scale
    exp_neg = jnp.exp(SCALE * dot_nt(query, keys))
    exp_pos = jnp.exp(positive)
    share = usable / (exp_pos + row_sum(exp_neg))
    d_pos = share * exp_pos - usable
    query_grad = SCALE * (
        dot((exp_neg * share).astype(BF), keys) + (d_pos * own_scale) * latent
    )
    target_grad_ref[...] = (SCALE * d_pos * own_scale) * query_f - (
        d_pos * positive * own_scale * own_scale
    ) * latent
    along = row_sum(unit * query_grad)
    pred_grad_ref[...] = (pred_scale * (query_grad - along * unit)).astype(BF)

    lane = lax.broadcasted_iota(jnp.int32, (BLOCK, 128), 1)
    columns = jnp.where(lane == 0, pred_scale, jnp.where(lane == 1, share, 0.0))
    rows = jnp.transpose(columns)[0:2]

    @pl.when(block == 0)
    def _():
        stats_ref[...] = jnp.zeros_like(stats_ref)

    for j in range(NEG):
        stats_ref[slot_ref[block * NEG + j]] = rows


def score(slots, answers, ctx, latents, levels, pred_weight, bd):
    rows = ctx.shape[0]
    count = answers.shape[0]
    whole = lambda *shape: pl.BlockSpec(shape, lambda i, s: (0,) * len(shape))
    rows_of = lambda width: pl.BlockSpec((BLOCK, width), lambda i, s: (i, 0))
    return pl.pallas_call(
        score_kernel,
        grid_spec=pltpu.PrefetchScalarGridSpec(
            num_scalar_prefetch=1,
            grid=(rows // BLOCK,),
            in_specs=[
                whole(count, PACK, 128), rows_of(256), rows_of(256), rows_of(128),
                whole(256, 256), whole(128, 1024),
            ],
            out_specs=(rows_of(256), rows_of(256), whole(count, 2, 128)),
        ),
        out_shape=(
            jax.ShapeDtypeStruct((rows, 256), BF),
            jax.ShapeDtypeStruct((rows, 256), F32),
            jax.ShapeDtypeStruct((count, 2, 128), F32),
        ),
        compiler_params=pltpu.CompilerParams(vmem_limit_bytes=40 * MIB),
        cost_estimate=pl.CostEstimate(
            flops=rows * 2 * 65536 * 10, bytes_accessed=16 * MIB, transcendentals=rows * 256 * 6
        ),
        name="score",
    )(slots, answers, ctx, latents, levels, pred_weight, bd)


def backward_kernel(pred_grad_ref, slope_ref, level_ref, target_grad_ref, rim_slope_ref,
                    rim_level_ref, pred_ref, w_ref, out_ref, rim_ref, carry):
    @pl.when(pl.program_id(0) == 0)
    def _():
        carry[...] = jnp.zeros_like(carry)

    def earlier(values, distance, place):
        longer = jnp.concatenate([values, carry[place]], axis=0)
        carry[place] = values[0:8]
        return longer[distance:distance + values.shape[0]]

    def through_layers(cotangent, slopes, level):
        for layer in reversed(range(LAYERS)):
            back = cotangent * slopes[layer].astype(F32)
            gated = jnp.where(level > layer, back, 0.0)
            cotangent = (
                cotangent
                + dot_nt(back.astype(BF), w_ref[layer, 0])
                + dot_nt(earlier(gated, 2**layer, layer).astype(BF), w_ref[layer, 1])
            )
        return cotangent

    context_rows = dot_nt(pred_grad_ref[...], pred_ref[...])
    cotangent = earlier(context_rows, AHEAD, LAYERS)
    level = jnp.broadcast_to(level_ref[:, 0:1], (SEGMENT, 256))
    out_ref[...] = through_layers(cotangent, slope_ref, level) + target_grad_ref[...]

    @pl.when(pl.program_id(0) == pl.num_programs(0) - 1)
    def _():
        cotangent = earlier(jnp.zeros((HALO, 256), F32), AHEAD, LAYERS)
        level = jnp.broadcast_to(rim_level_ref[:, 0:1], (HALO, 256))
        rim_ref[...] = through_layers(cotangent, rim_slope_ref, level)


def backward(pred_grad, slopes, levels, target_grad, rim_slopes, rim_levels, pred_weight, weight):
    rows = pred_grad.shape[0]
    steps = rows // SEGMENT
    whole = lambda *shape: pl.BlockSpec(shape, lambda i: (0,) * len(shape))
    rows_of = lambda width: pl.BlockSpec((SEGMENT, width), lambda i: (steps - 1 - i, 0))
    return pl.pallas_call(
        backward_kernel,
        grid=(steps,),
        out_shape=(
            jax.ShapeDtypeStruct((rows, 256), F32),
            jax.ShapeDtypeStruct((HALO, 256), F32),
        ),
        in_specs=[
            rows_of(256),
            pl.BlockSpec((LAYERS, SEGMENT, 256), lambda i: (0, steps - 1 - i, 0)),
            rows_of(128),
            rows_of(256),
            whole(LAYERS, HALO, 256),
            whole(HALO, 128),
            whole(256, 256),
            whole(LAYERS, 2, 256, 256),
        ],
        out_specs=(rows_of(256), whole(HALO, 256)),
        scratch_shapes=[pltpu.VMEM((LAYERS + 1, 8, 256), F32)],
        compiler_params=pltpu.CompilerParams(vmem_limit_bytes=40 * MIB),
        cost_estimate=pl.CostEstimate(
            flops=rows * 2 * 65536 * 9, bytes_accessed=22 * MIB, transcendentals=0
        ),
        name="backward",
    )(pred_grad, slopes, levels, target_grad, rim_slopes, rim_levels, pred_weight, weight)


def own_kernel(order_ref, count_ref, wanted_ref, ctx_ref, stats_ref, keyed_ref, part_ref, lat_ref,
               borrowed_ref, pred_ref, out_ref, total):
    step = pl.program_id(0)
    request_steps = order_ref.shape[0] // TOGETHER

    @pl.when(step == 0)
    def _():
        total[...] = jnp.zeros_like(total)

    @pl.when((step < request_steps) & (step * TOGETHER < count_ref[0]))
    def _():
        for j in range(TOGETHER):
            at = step * TOGETHER + j
            slot = order_ref[at]
            block = jnp.maximum(wanted_ref[slot], 0)
            rows = pl.ds(pl.multiple_of(block * BLOCK, BLOCK), BLOCK)
            stats = stats_ref[slot]
            pred_scale, share = stats[0:1], stats[1:2]
            scores = dot_nt(keyed_ref[rows, :], ctx_ref[j]) * (SCALE * pred_scale)
            weighted = jnp.exp(scores) * (share * pred_scale)
            weighted = jnp.where(at < count_ref[0], weighted, 0.0)
            total[rows, :] += dot(weighted.astype(BF), ctx_ref[j])

    @pl.when(step >= request_steps)
    def _():
        chunk = step - request_steps
        rows = pl.ds(pl.multiple_of(chunk * SEGMENT, SEGMENT), SEGMENT)
        direct = SCALE * dot(total[rows, :].astype(BF), pred_ref[...])
        latent = lat_ref[...].astype(F32)
        key_scale = lax.rsqrt(row_sum(latent * latent) + EPSILON)
        key = latent * key_scale
        out_ref[...] = part_ref[...] + key_scale * (direct - row_sum(key * direct) * key)

        @pl.when(step == pl.num_programs(0) - 1)
        def _():
            out_ref[SEGMENT - HALO:, :] += borrowed_ref[...]


def own(order, count, wanted, ctx, stats, keyed, part, latents, borrowed, pred_weight):
    rows = part.shape[0]
    slots = ctx.shape[0]
    request_steps = slots // TOGETHER
    whole = lambda *shape: pl.BlockSpec(shape, lambda i, o, c, w: (0,) * len(shape))
    chunk_of = pl.BlockSpec(
        (SEGMENT, 256), lambda i, o, c, w: (jnp.maximum(i - request_steps, 0), 0)
    )
    return pl.pallas_call(
        own_kernel,
        grid_spec=pltpu.PrefetchScalarGridSpec(
            num_scalar_prefetch=3,
            grid=(request_steps + rows // SEGMENT,),
            in_specs=[
                pl.BlockSpec(
                    (TOGETHER, BLOCK, 256),
                    lambda i, o, c, w: (jnp.minimum(i, last_step(c)), 0, 0),
                ),
                whole(slots, 2, 128),
                whole(rows, 256),
                chunk_of,
                chunk_of,
                whole(HALO, 256),
                whole(256, 256),
            ],
            out_specs=chunk_of,
            scratch_shapes=[pltpu.VMEM((rows, 256), F32)],
        ),
        out_shape=jax.ShapeDtypeStruct((rows, 256), F32),
        compiler_params=pltpu.CompilerParams(vmem_limit_bytes=40 * MIB),
        name="own",
    )(order, count, wanted, ctx, stats, keyed, part, latents, borrowed, pred_weight)


def shifted(block, axis, distance):
    devices = range(lax.axis_size(axis))
    route = [(i - distance, i) for i in devices if i - distance in devices]
    return lax.ppermute(block, axis, route)


def exchanged(slots):
    owners_count = slots.shape[0] // CAP
    sent = slots.reshape((owners_count, CAP) + slots.shape[1:])
    got = lax.all_to_all(sent, ("tm", "stream"), split_axis=0, concat_axis=0, tiled=True)
    return got.reshape(slots.shape)


def body(raw, starts, neg_owner, neg_block, enc_weight, tcn_weight, pred_weight):
    raw = raw[0]
    owners_count = lax.axis_size("tm") * lax.axis_size("stream")
    rim_starts = jnp.zeros((2, 128), BF).at[0, 128 - HALO:].set(starts[0, -HALO:].astype(BF))
    rim = shifted(jnp.concatenate([raw[:, -128:], rim_starts], axis=0), "tm", 1)
    half_weight = (tcn_weight * 0.5).astype(BF)
    pack, push, slots, bd = prep(
        neg_owner.reshape(-1), neg_block.reshape(-1), raw, starts.reshape(-1, BLOCK), rim,
        enc_weight, owners_count,
    )
    pushed = exchanged(push)
    latents, ctx, slopes, levels, rim_slopes, rim_levels, keyed = forward(
        pack, bd, half_weight, pred_weight
    )
    wanted = pushed[:, PACK - 1, 64].astype(jnp.int32)
    replies, order, count = answer(wanted, pack)
    answers = exchanged(replies)
    request_ctx = recompute(order, count, pushed, bd, half_weight)
    pred_grad, target_grad, stats = score(slots, answers, ctx, latents, levels, pred_weight, bd)
    got_stats = exchanged(stats)
    part, rim_grad = backward(
        pred_grad, slopes, levels, target_grad, rim_slopes, rim_levels, pred_weight, tcn_weight
    )
    borrowed = shifted(rim_grad, "tm", -1)
    return own(
        order, count, wanted, request_ctx, got_stats, keyed, part, latents, borrowed, pred_weight
    )[None]


def solution(mesh):
    placed = (
        P("stream", None, "tm"),
        P("stream", "tm"),
        P("stream", "tm", None),
        P("stream", "tm", None),
        P(),
        P(),
        P(),
    )
    return jax.shard_map(
        body, mesh=mesh, in_specs=placed, out_specs=P("stream", "tm", None), check_vma=False
    )
```

time: 735 us -> 342 us (0.47)
  the two profiles are of different devices: /device:TPU:10 before, /device:TPU:88 now
where the time goes in v1:
time: 342 us; the launch traced here: 339 us
  Pallas kernels  236 us (69%)
  local copies, waits for them, and re-layouts  34.8 us (10%)
  blocking collectives  33.1 us (10%)
  starting transfers between devices  24.1 us (7%)
  other arithmetic  7.64 us (2%)
    pallas_call x1, Pallas kernels, recompute(): pl.pallas_call(recompute_kernel, grid_spec=pltpu.PrefetchScalarGridSpec(n...  123 us
    pallas_call x1, Pallas kernels, own(): pl.pallas_call(own_kernel, grid_spec=pltpu.PrefetchScalarGridSpec(num_sca...  35.7 us
    pallas_call x1, Pallas kernels, score(): pl.pallas_call(score_kernel, grid_spec=pltpu.PrefetchScalarGridSpec(num_s...  34 us
    all_to_all x1, blocking collectives, exchanged(): lax.all_to_all(sent, ('tm', 'stream'), split_axis=0, concat_axis=0, tiled...  33.1 us
    unnamed x68, local copies, waits for them, and re-layouts  31.8 us
    pallas_call x1, Pallas kernels, forward(): pl.pallas_call(forward_kernel, grid=(steps,), out_shape=(jax.ShapeDtypeSt...  19.3 us
    all_to_all x2, starting transfers between devices, exchanged(): lax.all_to_all(sent, ('tm', 'stream'), split_axis=0, concat_axis=0, tiled...  17.6 us
    pallas_call x1, Pallas kernels, backward(): pl.pallas_call(backward_kernel, grid=(steps,), out_shape=(jax.ShapeDtypeS...  13.7 us
  transfers between devices with their start and end apart: 4, of which 1 were waited for; matrix products, arithmetic and copies ran while one was open for 1% of the time, Pallas kernels for 42%

profile of v1, /device:TPU:88, one launch (start us, length us, event | category | flops | bytes accessed | tf_op | source)
XLA Modules:
  0.0 339.2 jit_solution(18364572726246987209)
XLA Ops:
  0.6 1.3 and_reduce_fusion
  2.6 1.4 broadcast_select_fusion
  4.0 1.5 scatter.4
  5.5 1.9 collective-permute-start
  9.2 3.3 collective-permute-done.rim_ref
  14.9 5.4 %prep.1 = (bf16[32,32,128]{2,1,0:T(8,128)(2,1)S(1)}, bf16[256,32,128]{2,1,0:T(8,128)(2,1)S(1)}, s32[128]{0:T(128)S(1)}, bf16[128,1024]{1,0:T(8,128)(2,1)S(1)}) custom-call(s32[128]{0:T(128)S(1)} %reshape.63.owner_ref, s32[128]{0:T(128)S(1)} %reshape.64.block_ref, bf16[6,16384]{1,0:T(8,128)(2,1)S(1)} %bitcast.17, s32[32,128]{1,0:T(8,128)S(1)} %bitcast.18, ...), custom_call_target="tpu_custom_call" | custom-call | tf_op jit(solution)/shard_map/prep/pallas_call | solution.py:120
  20.3 33.1 %all_to_all.15 = bf16[128,2,32,128]{3,2,1,0:T(8,128)(2,1)S(1)} all-to-all(bf16[128,2,32,128]{3,2,1,0:T(8,128)(2,1)S(1)} %bitcast.14), channel_id=1, replica_groups=mesh['tm'=32,'stream'=4] {'tm','stream'}, dimensions={0} | all-to-all | bytes 4194304 | tf_op jit(solution)/shard_map/all_to_all | solution.py:545
  53.4 4.9 %fusion.wanted_ref = s32[256]{0:T(256)S(1)} fusion(bf16[256,32,128]{2,1,0:T(8,128)(2,1)S(1)} %bitcast.11), kind=kLoop, calls=%fused_computation.2 | loop fusion | flops 256 | bytes 1536 | tf_op jit(solution)/shard_map/convert_element_type | solution.py:563
  58.3 4.8 %answer.1 = (bf16[256,32,128]{2,1,0:T(8,128)(2,1)S(1)}, s32[256]{0:T(256)S(1)}, s32[1]{0:T(128)}) custom-call(s32[256]{0:T(256)S(1)} %fusion.wanted_ref, bf16[32,32,128]{2,1,0:T(8,128)(2,1)S(1)} %get-tuple-element.37.pack_ref), custom_call_target="tpu_custom_call" | custom-call | tf_op jit(solution)/shard_map/answer/pallas_call | solution.py:257
  63.1 1.3 copy-done.12
  65.0 10.2 %all-to-all-start.1 = ((bf16[128,2,32,128]{3,2,1,0:T(8,128)(2,1)}), bf16[128,2,32,128]{3,2,1,0:T(8,128)(2,1)}, u32[]{:S(2)}, u32[]{:S(2)}) async-start(bf16[128,2,32,128]{3,2,1,0:T(8,128)(2,1)} %bitcast.13), calls=%async_computation.1 | async-start | bytes 4194304 | tf_op jit(solution)/shard_map/all_to_all | solution.py:545
  76.2 19.3 %forward.1 = (bf16[4096,256]{1,0:T(8,128)(2,1)S(1)}, bf16[4096,256]{1,0:T(8,128)(2,1)S(1)}, bf16[4,4096,256]{2,1,0:T(8,128)(2,1)}, f32[4096,128]{1,0:T(8,128)S(1...) custom-call(bf16[32,32,128]{2,1,0:T(8,128)(2,1)S(1)} %get-tuple-element.37.pack_ref, ...), custom_call_target="tpu_custom_call" | custom-call | flops 5368709120 | bytes 18874368 | tf_op jit(solution)/shard_map/forward/pallas_call | solution.py:199
  95.5 1.4 copy-done.4
  96.9 1.3 copy-done.7
  98.2 1.4 copy-done.9
  99.6 1.0 copy-done.13
  101.2 1.3 copy-done.31
  102.5 1.6 copy-done.5
  104.1 1.6 copy-done.10
  107.3 1.6 copy-done.32
  108.9 34.0 %score.1 = (bf16[4096,256]{1,0:T(8,128)(2,1)S(1)}, f32[4096,256]{1,0:T(8,128)}, f32[256,2,128]{2,1,0:T(2,128)}) custom-call(s32[128]{0:T(128)S(1)} %copy-done.30, bf16[256,32,128]{2,1,0:T(8,128)(2,1)} %bitcast.7.answer_ref, bf16[4096,256]{1,0:T(8,128)(2,1)S(1)} %copy-done.32, bf16[4096,256]{1,0:T(8,128)(2,1)S(1)} %copy-done.5, f32[4096,128]{1,0:T(8,128)S(1)} %copy-done.10, ...), custom_call_target="tpu_custom_call" | custom-call | flops 5368709120 | bytes 16777216 | tf_op jit(solution)/shard_map/score/pallas_call | solution.py:374
  142.9 2.2 copy-done.2
  145.1 13.7 %backward.1 = (f32[4096,256]{1,0:T(8,128)S(1)}, f32[32,256]{1,0:T(8,128)S(1)}) custom-call(bf16[4096,256]{1,0:T(8,128)(2,1)S(1)} %get-tuple-element.48.pred_grad_ref, bf16[4,4096,256]{2,1,0:T(8,128)(2,1)} %get-tuple-element.49.slope_ref, f32[4096,128]{1,0:T(8,128)S(1)} %copy-done.11, f32[4096,256]{1,0:T(8,128)S(1)} %copy-done.2, ...), custom_call_target="tpu_custom_call" | custom-call | flops 4831838208 | bytes 23068672 | tf_op jit(solution)/shard_map/backward/pallas_call | solution.py:437
  158.8 2.0 copy-done
  160.8 4.6 %collective-permute-start.1 = (f32[32,256]{1,0:T(8,128)S(1)}, f32[32,256]{1,0:T(8,128)S(1)}, u32[]{:S(2)}, u32[]{:S(2)}) collective-permute-start(f32[32,256]{1,0:T(8,128)S(1)} %get-tuple-element.54), channel_id=1, source_target_pairs={{4,0},{8,4},{12,8},{16,12},{20,16},{24,20},{28,24},{32,28},{36,32}... | collective-permute-start | bytes 98312 | tf_op jit(solution)/shard_map/ppermute | solution.py:539
  165.4 7.4 %all-to-all-start.2 = ((f32[128,2,2,128]{3,2,1,0:T(2,128)}), f32[128,2,2,128]{3,2,1,0:T(2,128)S(1)}, u32[]{:S(2)}, u32[]{:S(2)}) async-start(f32[128,2,2,128]{3,2,1,0:T(2,128)} %bitcast.8), calls=%async_computation.2 | async-start | bytes 524288 | tf_op jit(solution)/shard_map/all_to_all | solution.py:545
  172.8 1.2 copy-done.14
  175.0 123.1 %recompute.1.ctx_ref = bf16[256,128,256]{2,1,0:T(8,128)(2,1)} custom-call(s32[256]{0:T(256)S(1)} %copy-done.24, s32[1]{0:T(128)} %get-tuple-element.39.count_ref, bf16[256,32,128]{2,1,0:T(8,128)(2,1)S(1)} %bitcast.12, bf16[128,1024]{1,0:T(8,128)(2,1)S(1)} %copy-done.28, bf16[4,2,256,256]{3,2,1,0:T(8,128)(2,1)S(1)} %copy-done.14), custom_call_target="tpu_custom_call" | custom-call | flops 53687091200 | bytes 20971520 | tf_op jit(solution)/shard_map/recompute/pallas_call | solution.py:302
  298.1 2.2 copy-done.1
  300.3 1.6 copy-done.6
  301.9 1.6 copy-done.8
  303.5 35.7 %own.1 = f32[4096,256]{1,0:T(8,128)} custom-call(s32[256]{0:T(256)S(1)} %copy-done.24, s32[1]{0:T(128)} %get-tuple-element.39.count_ref, s32[256]{0:T(256)S(1)} %copy-done.22, bf16[256,128,256]{2,1,0:T(8,128)(2,1)} %recompute.1.ctx_ref, f32[256,2,128]{2,1,0:T(2,128)S(1)} %bitcast.15, bf16[4096,256]{1,0:T(8,128)(2,1)S(1)} %copy-done.8, ...), custom_call_target="tpu_custom_call" | custom-call | tf_op jit(solution)/shard_map/own/pallas_call | solution.py:510
  (64 shorter events, 10.3 us)
Async XLA Ops:
  5.5 7.0 %collective-permute-start = (bf16[8,128]{1,0:T(8,128)(2,1)S(1)}, bf16[8,128]{1,0:T(8,128)(2,1)S(1)}, u32[]{:S(2)}, u32[]{:S(2)}) collective-permute-start(bf16[8,128]{1,0:T(8,128)(2,1)S(1)} %pad_maximum_fusion), channel_id=1, source_target_pairs={{0,4},{4,8},{8,12},{12,16},{16,20},{20,24},{24,28},{28,32},{32,36}... | collective-permute-start | bytes 6152 | tf_op jit(solution)/shard_map/ppermute | solution.py:539
  12.5 1.0 copy-start.16
  20.3 33.1 %copy-start.25 = (bf16[128,1024]{1,0:T(8,128)(2,1)}, bf16[128,1024]{1,0:T(8,128)(2,1)S(1)}, u32[]{:S(2)}) copy-start(bf16[128,1024]{1,0:T(8,128)(2,1)S(1)} %get-tuple-element.40.bd_ref) | copy-start | bytes 786436
  20.3 33.1 %copy-start.29 = (s32[128]{0:T(128)}, s32[128]{0:T(128)S(1)}, u32[]{:S(2)}) copy-start(s32[128]{0:T(128)S(1)} %get-tuple-element.41.slot_ref) | copy-start | bytes 1540
  58.2 6.1 %copy-start.21 = (s32[256]{0:T(256)}, s32[256]{0:T(256)S(1)}, u32[]{:S(2)}) copy-start(s32[256]{0:T(256)S(1)} %fusion.wanted_ref) | copy-start | bytes 3076
  63.0 1.3 copy-start.12
  65.0 10.2 %copy-start.3 = (bf16[4,2,256,256]{3,2,1,0:T(8,128)(2,1)S(1)}, bf16[4,2,256,256]{3,2,1,0:T(8,128)(2,1)}, u32[]{:S(2)}) copy-start(bf16[4,2,256,256]{3,2,1,0:T(8,128)(2,1)} %w_ref.1) | copy-start | bytes 3145732
  65.0 37.5 %all-to-all-start.1 = ((bf16[128,2,32,128]{3,2,1,0:T(8,128)(2,1)}), bf16[128,2,32,128]{3,2,1,0:T(8,128)(2,1)}, u32[]{:S(2)}, u32[]{:S(2)}) async-start(bf16[128,2,32,128]{3,2,1,0:T(8,128)(2,1)} %bitcast.13), calls=%async_computation.1 | async-start | bytes 4194304 | tf_op jit(solution)/shard_map/all_to_all | solution.py:545
  75.2 0.9 copy-start.15
  75.2 1.0 copy-start.26
  95.5 1.4 copy-start.4
  96.9 1.3 copy-start.7
  98.2 1.4 copy-start.9
  99.6 1.0 copy-start.13
  101.1 1.3 copy-start.31
  102.5 1.6 copy-start.5
  104.0 1.6 copy-start.10
  105.6 0.9 copy-start.27
  107.3 1.6 copy-start.32
  108.9 34.0 %copy-start.11 = (f32[4096,128]{1,0:T(8,128)S(1)}, f32[4096,128]{1,0:T(8,128)}, u32[]{:S(2)}) copy-start(f32[4096,128]{1,0:T(8,128)} %copy-done.9) | copy-start | bytes 6291460
  108.9 34.0 %copy-start.18 = (bf16[4,32,256]{2,1,0:T(8,128)(2,1)S(1)}, bf16[4,32,256]{2,1,0:T(8,128)(2,1)}, u32[]{:S(2)}) copy-start(bf16[4,32,256]{2,1,0:T(8,128)(2,1)} %copy-done.17) | copy-start | bytes 196612
  142.9 2.2 copy-start.2
  145.1 27.7 %copy-start.24 = (s32[256]{0:T(256)S(1)}, s32[256]{0:T(256)}, u32[]{:S(2)}) copy-start(s32[256]{0:T(256)} %copy-done.23) | copy-start | bytes 3076
  158.8 2.0 copy-start
  160.8 137.3 %collective-permute-start.1 = (f32[32,256]{1,0:T(8,128)S(1)}, f32[32,256]{1,0:T(8,128)S(1)}, u32[]{:S(2)}, u32[]{:S(2)}) collective-permute-start(f32[32,256]{1,0:T(8,128)S(1)} %get-tuple-element.54), channel_id=1, source_target_pairs={{4,0},{8,4},{12,8},{16,12},{20,16},{24,20},{28,24},{32,28},{36,32}... | collective-permute-start | bytes 98312 | tf_op jit(solution)/shard_map/ppermute | solution.py:539
  165.4 132.7 %all-to-all-start.2 = ((f32[128,2,2,128]{3,2,1,0:T(2,128)}), f32[128,2,2,128]{3,2,1,0:T(2,128)S(1)}, u32[]{:S(2)}, u32[]{:S(2)}) async-start(f32[128,2,2,128]{3,2,1,0:T(2,128)} %bitcast.8), calls=%async_computation.2 | async-start | bytes 524288 | tf_op jit(solution)/shard_map/all_to_all | solution.py:545
  172.8 1.2 copy-start.14
  174.0 0.9 copy-start.28
  175.0 123.1 %copy-start.22 = (s32[256]{0:T(256)S(1)}, s32[256]{0:T(256)}, u32[]{:S(2)}) copy-start(s32[256]{0:T(256)} %copy-done.21) | copy-start | bytes 3076
  298.1 2.2 copy-start.1
  300.3 1.6 copy-start.6
  301.9 1.6 copy-start.8
  (5 other events, 3.3 us)

commit v2 on v1

--- a/solution.py
+++ b/solution.py
@@ -12,13 +12,16 @@
 CAP = 2
 LAYERS = 4
 PACK = 32
-TOGETHER = 8
+TOGETHER = 16
+LEAD = 20
 SEGMENT = 512
+SCORED = 4
 SCALE = 10.0
 EPSILON = 1e-06
 BF = jnp.bfloat16
 F32 = jnp.float32
 MIB = 1 << 20
+VMEM = 60 * MIB
 
 
 def dot(a, b):
@@ -132,7 +135,7 @@
             pltpu.VMEM((blocks, PACK, 128), F32),
             pltpu.SMEM((owners_count,), jnp.int32),
         ],
-        compiler_params=pltpu.CompilerParams(vmem_limit_bytes=32 * MIB),
+        compiler_params=pltpu.CompilerParams(vmem_limit_bytes=VMEM),
         name="prep",
     )(owners, wanted, raw, starts, rim, enc_weight)
 
@@ -223,7 +226,7 @@
             whole(HALO, 128),
             rows_of(256),
         ),
-        compiler_params=pltpu.CompilerParams(vmem_limit_bytes=40 * MIB),
+        compiler_params=pltpu.CompilerParams(vmem_limit_bytes=VMEM),
         cost_estimate=pl.CostEstimate(
             flops=rows * 2 * 65536 * 10, bytes_accessed=18 * MIB, transcendentals=rows * 256 * 5
         ),
@@ -231,65 +234,108 @@
     )(pack, bd, half_weight, pred_weight)
 
 
-def answer_kernel(wanted_ref, pack_ref, answer_ref, order_ref, count_ref):
-    slots = wanted_ref.shape[0]
+def answer_kernel(push_ref, pack_ref, answer_ref, order_ref, count_ref, wanted_ref, listed, arrived):
+    slots = push_ref.shape[0]
+    notes = push_ref[:, PACK - 16:, :].astype(F32)[:, 15, :]
+    listed[...] = jnp.transpose(notes)[64:72].astype(jnp.int32)
+    pltpu.sync_copy(listed, arrived)
 
     def clear(i, carry):
         order_ref[i] = 0
         return carry
 
-    lax.fori_loop(0, slots, clear, 0)
+    lax.fori_loop(0, slots, clear, 0, unroll=8)
 
     def reply(i, count):
-        wanted = wanted_ref[i]
+        wanted = arrived[0, i]
+        wanted_ref[i] = jnp.maximum(wanted, 0)
         answer_ref[i] = pack_ref[jnp.maximum(wanted, 0)]
         order_ref[count] = i
         return count + jnp.where(wanted >= 0, 1, 0)
 
-    count = lax.fori_loop(0, slots, reply, 0)
+    count = lax.fori_loop(0, slots, reply, 0, unroll=8)
     count_ref[0] = count
 
 
-def answer(wanted, pack):
-    slots = wanted.shape[0]
+def answer(pushed, pack):
+    slots = pushed.shape[0]
     smem = pl.BlockSpec(memory_space=pltpu.SMEM)
     vmem = pl.BlockSpec(memory_space=pltpu.VMEM)
     return pl.pallas_call(
         answer_kernel,
         out_shape=(
             jax.ShapeDtypeStruct((slots, PACK, 128), BF),
+            jax.ShapeDtypeStruct((slots + 8,), jnp.int32),
+            jax.ShapeDtypeStruct((1,), jnp.int32),
             jax.ShapeDtypeStruct((slots,), jnp.int32),
-            jax.ShapeDtypeStruct((1,), jnp.int32),
-        ),
-        in_specs=[smem, vmem],
-        out_specs=(vmem, smem, smem),
-        compiler_params=pltpu.CompilerParams(vmem_limit_bytes=16 * MIB),
+        ),
+        in_specs=[vmem, vmem],
+        out_specs=(vmem, smem, smem, smem),
+        scratch_shapes=[pltpu.VMEM((8, slots), jnp.int32), pltpu.SMEM((8, slots), jnp.int32)],
+        compiler_params=pltpu.CompilerParams(vmem_limit_bytes=VMEM),
         name="answer",
-    )(wanted, pack)
-
-
-def recompute_kernel(order_ref, count_ref, push_ref, bd_ref, w_ref, ctx_ref):
+    )(pushed, pack)
+
+
+def halo_rows(turned):
+    lane = lax.broadcasted_iota(jnp.int32, (HALO, 128), 1) & 31
+    halo = jnp.where(lane == 30, pltpu.roll(turned[0:HALO], 127, 1), 0.0)
+    for k in range(4):
+        moved = pltpu.roll(turned[k * 32:(k + 1) * 32], (6 * k - 24) % 128, 1)
+        halo = jnp.where((lane >= 6 * k) & (lane < 6 * k + 6), moved, halo)
+    return halo
+
+
+def recompute_kernel(order_ref, count_ref, push_ref, bd_ref, w_ref, ctx_ref,
+                     patches, level, here, there, left, right):
     base = pl.program_id(0) * TOGETHER
+    times = LEAD + BLOCK - AHEAD
 
     @pl.when(base < count_ref[0])
     def _():
-        bd = bd_ref[...]
-        hidden, levels = [], []
         for part in range(TOGETHER // 4):
             turned = turn([push_ref[order_ref[base + part * 4 + q]] for q in range(4)])
-            encoded = encode_with_halo(turned, bd)
+            halo = halo_rows(turned)
             for q in range(4):
-                hidden.append(encoded[128:160, q * 256:(q + 1) * 256])
-                hidden.append(encoded[0:128, q * 256:(q + 1) * 256])
-                levels.append(turned[0:32, q * 32 + 31:q * 32 + 32])
-                levels.append(turned[:, q * 32 + 30:q * 32 + 31])
-        h = jnp.concatenate(hidden, axis=0)
-        level = jnp.broadcast_to(jnp.concatenate(levels, axis=0), h.shape)
+                j = part * 4 + q
+                shift = (-32 * q) % 128
+                own = pltpu.roll(turned, shift, 1) if q else turned
+                before = pltpu.roll(halo, shift, 1) if q else halo
+                patches[pl.ds(j, LEAD, stride=TOGETHER), :] = before[HALO - LEAD:]
+                patches[pl.ds(LEAD * TOGETHER + j, BLOCK - AHEAD, stride=TOGETHER), :] = own[:BLOCK - AHEAD]
+        enc = bd_ref[:, 0:256]
+        row = lax.broadcasted_iota(jnp.int32, (128, 128), 0)
+        pick = jnp.where(row == 30, 1.0, 0.0).astype(BF)
+
+        def pieces(first, parts):
+            edges = [first + (times - first) * p // parts for p in range(parts + 1)]
+            return [(a * TOGETHER, b * TOGETHER) for a, b in zip(edges[:-1], edges[1:])]
+
+        for a, b in pieces(0, 4):
+            x = patches[a:b, :].astype(BF)
+            here[a:b, :] = silu_of_half(dot(x, enc)).astype(BF)
+            level[a:b, :] = dot(x, pick).astype(BF)
+        source, target = here, there
+        first = 0
         for layer in range(LAYERS):
-            h = h + silu_of_half(layer_half(h, level, layer, w_ref))
+            first += 2**layer if layer else 2
+            back = 2**layer * TOGETHER
+            for a, b in pieces(first, 4):
+                h = source[a:b, :]
+                gate = jnp.minimum(jnp.maximum(level[a:b, :] - float(layer), 0.0), 1.0)
+                gated = source[a - back:b - back, :] * jnp.concatenate([gate, gate], axis=1)
+                half = dot(h, w_ref[layer, 0]) + dot(gated, w_ref[layer, 1])
+                result = h.astype(F32) + silu_of_half(half)
+                if layer < LAYERS - 1:
+                    target[a:b, :] = result.astype(BF)
+                else:
+                    at = first * TOGETHER
+                    left[a - at:b - at, :] = result[:, 0:128]
+                    right[a - at:b - at, :] = result[:, 128:256]
+            source, target = target, source
         for j in range(TOGETHER):
-            at = j * (HALO + BLOCK) + HALO - AHEAD
-            ctx_ref[j] = h[at:at + BLOCK].astype(BF)
+            rows = pl.ds(j, BLOCK, stride=TOGETHER)
+            ctx_ref[j] = jnp.concatenate([left[rows, :], right[rows, :]], axis=1).astype(BF)
 
 
 def last_step(count_ref):
@@ -298,6 +344,7 @@
 
 def recompute(order, count, pushed, bd, half_weight):
     slots = pushed.shape[0]
+    times = LEAD + BLOCK - AHEAD
     whole = lambda *shape: pl.BlockSpec(shape, lambda i, o, c: (0,) * len(shape))
     return pl.pallas_call(
         recompute_kernel,
@@ -308,9 +355,17 @@
             out_specs=pl.BlockSpec(
                 (TOGETHER, BLOCK, 256), lambda i, o, c: (jnp.minimum(i, last_step(c)), 0, 0)
             ),
+            scratch_shapes=[
+                pltpu.VMEM((times * TOGETHER, 128), F32),
+                pltpu.VMEM((times * TOGETHER, 128), BF),
+                pltpu.VMEM((times * TOGETHER, 256), BF),
+                pltpu.VMEM((times * TOGETHER, 256), BF),
+                pltpu.VMEM((BLOCK * TOGETHER, 128), F32),
+                pltpu.VMEM((BLOCK * TOGETHER, 128), F32),
+            ],
         ),
         out_shape=jax.ShapeDtypeStruct((slots, BLOCK, 256), BF),
-        compiler_params=pltpu.CompilerParams(vmem_limit_bytes=48 * MIB),
+        compiler_params=pltpu.CompilerParams(vmem_limit_bytes=VMEM),
         cost_estimate=pl.CostEstimate(
             flops=slots * 160 * 2 * 65536 * 10, bytes_accessed=20 * MIB,
             transcendentals=slots * 160 * 256 * 5,
@@ -319,63 +374,70 @@
     )(order, count, pushed, bd, half_weight)
 
 
+def square_sums(x):
+    return dot((x * x).astype(BF), jnp.ones((256, 128), BF))
+
+
 def score_kernel(slot_ref, answer_ref, ctx_ref, lat_ref, level_ref, pred_ref, bd_ref,
                  pred_grad_ref, target_grad_ref, stats_ref):
-    block = pl.program_id(0)
-    raw_pred = dot(ctx_ref[...], pred_ref[...])
-    pred_scale = lax.rsqrt(row_sum(raw_pred * raw_pred) + EPSILON)
-    unit = raw_pred * pred_scale
-    query = unit.astype(BF)
-    query_f = query.astype(F32)
-
-    turned = turn([answer_ref[slot_ref[block * NEG + j]] for j in range(NEG)])
-    encoded = silu_of_half(dot(turned.astype(BF), bd_ref[...]))
-    keys = []
-    for j in range(NEG):
-        negative = encoded[:, j * 256:(j + 1) * 256]
-        key_scale = lax.rsqrt(row_sum(negative * negative) + EPSILON)
-        keys.append((negative * key_scale).astype(BF))
-    keys = jnp.concatenate(keys, axis=0)
-
-    latent = lat_ref[...].astype(F32)
-    usable = jnp.where(level_ref[:, 0:1] > 2.0, 1.0, 0.0)
-    own_scale = lax.rsqrt(row_sum(latent * latent) + EPSILON)
-    positive = SCALE * row_sum(query_f * latent) * own_scale
-    exp_neg = jnp.exp(SCALE * dot_nt(query, keys))
-    exp_pos = jnp.exp(positive)
-    share = usable / (exp_pos + row_sum(exp_neg))
-    d_pos = share * exp_pos - usable
-    query_grad = SCALE * (
-        dot((exp_neg * share).astype(BF), keys) + (d_pos * own_scale) * latent
-    )
-    target_grad_ref[...] = (SCALE * d_pos * own_scale) * query_f - (
-        d_pos * positive * own_scale * own_scale
-    ) * latent
-    along = row_sum(unit * query_grad)
-    pred_grad_ref[...] = (pred_scale * (query_grad - along * unit)).astype(BF)
-
+    step = pl.program_id(0)
+
+    @pl.when(step == 0)
+    def _():
+        stats_ref[...] = jnp.zeros_like(stats_ref)
+
+    slots = [slot_ref[step * SCORED * NEG + i] for i in range(SCORED * NEG)]
     lane = lax.broadcasted_iota(jnp.int32, (BLOCK, 128), 1)
-    columns = jnp.where(lane == 0, pred_scale, jnp.where(lane == 1, share, 0.0))
-    rows = jnp.transpose(columns)[0:2]
-
-    @pl.when(block == 0)
-    def _():
-        stats_ref[...] = jnp.zeros_like(stats_ref)
-
-    for j in range(NEG):
-        stats_ref[slot_ref[block * NEG + j]] = rows
+    raw_preds = dot(ctx_ref[...], pred_ref[...])
+    for g in range(SCORED):
+        at = slice(g * BLOCK, (g + 1) * BLOCK)
+        raw_pred = raw_preds[at]
+        pred_scale = lax.rsqrt(row_sum(raw_pred * raw_pred) + EPSILON)
+        unit = raw_pred * pred_scale
+        query = unit.astype(BF)
+        query_f = query.astype(F32)
+
+        turned = turn([answer_ref[slots[g * NEG + j]] for j in range(NEG)])
+        encoded = silu_of_half(dot(turned.astype(BF), bd_ref[...]))
+        keys = []
+        for j in range(NEG):
+            negative = encoded[:, j * 256:(j + 1) * 256]
+            key_scale = lax.rsqrt(square_sums(negative) + EPSILON)
+            keys.append((negative * jnp.concatenate([key_scale, key_scale], axis=1)).astype(BF))
+        keys = jnp.concatenate(keys, axis=0)
+
+        latent = lat_ref[at, :].astype(F32)
+        usable = jnp.where(level_ref[at, 0:1] > 2.0, 1.0, 0.0)
+        own_scale = lax.rsqrt(row_sum(latent * latent) + EPSILON)
+        positive = SCALE * row_sum(query_f * latent) * own_scale
+        exp_neg = jnp.exp(SCALE * dot_nt(query, keys))
+        exp_pos = jnp.exp(positive)
+        share = usable / (exp_pos + row_sum(exp_neg))
+        d_pos = share * exp_pos - usable
+        query_grad = SCALE * (
+            dot((exp_neg * share).astype(BF), keys) + (d_pos * own_scale) * latent
+        )
+        target_grad_ref[at, :] = (SCALE * d_pos * own_scale) * query_f - (
+            d_pos * positive * own_scale * own_scale
+        ) * latent
+        along = row_sum(unit * query_grad)
+        pred_grad_ref[at, :] = (pred_scale * (query_grad - along * unit)).astype(BF)
+        columns = jnp.where(lane == 0, pred_scale, jnp.where(lane == 1, share, 0.0))
+        rows = jnp.transpose(columns)[0:2]
+        for j in range(NEG):
+            stats_ref[slots[g * NEG + j]] = rows
 
 
 def score(slots, answers, ctx, latents, levels, pred_weight, bd):
     rows = ctx.shape[0]
     count = answers.shape[0]
     whole = lambda *shape: pl.BlockSpec(shape, lambda i, s: (0,) * len(shape))
-    rows_of = lambda width: pl.BlockSpec((BLOCK, width), lambda i, s: (i, 0))
+    rows_of = lambda width: pl.BlockSpec((SCORED * BLOCK, width), lambda i, s: (i, 0))
     return pl.pallas_call(
         score_kernel,
         grid_spec=pltpu.PrefetchScalarGridSpec(
             num_scalar_prefetch=1,
-            grid=(rows // BLOCK,),
+            grid=(rows // BLOCK // SCORED,),
             in_specs=[
                 whole(count, PACK, 128), rows_of(256), rows_of(256), rows_of(128),
                 whole(256, 256), whole(128, 1024),
@@ -387,7 +449,7 @@
             jax.ShapeDtypeStruct((rows, 256), F32),
             jax.ShapeDtypeStruct((count, 2, 128), F32),
         ),
-        compiler_params=pltpu.CompilerParams(vmem_limit_bytes=40 * MIB),
+        compiler_params=pltpu.CompilerParams(vmem_limit_bytes=VMEM),
         cost_estimate=pl.CostEstimate(
             flops=rows * 2 * 65536 * 10, bytes_accessed=16 * MIB, transcendentals=rows * 256 * 6
         ),
@@ -453,7 +515,7 @@
         ],
         out_specs=(rows_of(256), whole(HALO, 256)),
         scratch_shapes=[pltpu.VMEM((LAYERS + 1, 8, 256), F32)],
-        compiler_params=pltpu.CompilerParams(vmem_limit_bytes=40 * MIB),
+        compiler_params=pltpu.CompilerParams(vmem_limit_bytes=VMEM),
         cost_estimate=pl.CostEstimate(
             flops=rows * 2 * 65536 * 9, bytes_accessed=22 * MIB, transcendentals=0
         ),
@@ -464,7 +526,7 @@
 def own_kernel(order_ref, count_ref, wanted_ref, ctx_ref, stats_ref, keyed_ref, part_ref, lat_ref,
                borrowed_ref, pred_ref, out_ref, total):
     step = pl.program_id(0)
-    request_steps = order_ref.shape[0] // TOGETHER
+    request_steps = pl.num_programs(0) - total.shape[0] // SEGMENT
 
     @pl.when(step == 0)
     def _():
@@ -472,17 +534,21 @@
 
     @pl.when((step < request_steps) & (step * TOGETHER < count_ref[0]))
     def _():
-        for j in range(TOGETHER):
-            at = step * TOGETHER + j
-            slot = order_ref[at]
-            block = jnp.maximum(wanted_ref[slot], 0)
-            rows = pl.ds(pl.multiple_of(block * BLOCK, BLOCK), BLOCK)
-            stats = stats_ref[slot]
-            pred_scale, share = stats[0:1], stats[1:2]
-            scores = dot_nt(keyed_ref[rows, :], ctx_ref[j]) * (SCALE * pred_scale)
-            weighted = jnp.exp(scores) * (share * pred_scale)
-            weighted = jnp.where(at < count_ref[0], weighted, 0.0)
-            total[rows, :] += dot(weighted.astype(BF), ctx_ref[j])
+        for part in range(0, TOGETHER, 4):
+            found = []
+            for j in range(part, part + 4):
+                at = step * TOGETHER + j
+                slot = order_ref[at]
+                block = wanted_ref[slot]
+                rows = pl.ds(pl.multiple_of(block * BLOCK, BLOCK), BLOCK)
+                stats = stats_ref[slot]
+                pred_scale, share = stats[0:1], stats[1:2]
+                scores = dot_nt(keyed_ref[rows, :], ctx_ref[j]) * (SCALE * pred_scale)
+                weighted = jnp.exp(scores) * (share * pred_scale)
+                weighted = jnp.where(at < count_ref[0], weighted, 0.0)
+                found.append((rows, dot(weighted.astype(BF), ctx_ref[j])))
+            for rows, addend in found:
+                total[rows, :] += addend
 
     @pl.when(step >= request_steps)
     def _():
@@ -528,7 +594,7 @@
             scratch_shapes=[pltpu.VMEM((rows, 256), F32)],
         ),
         out_shape=jax.ShapeDtypeStruct((rows, 256), F32),
-        compiler_params=pltpu.CompilerParams(vmem_limit_bytes=40 * MIB),
+        compiler_params=pltpu.CompilerParams(vmem_limit_bytes=VMEM),
         name="own",
     )(order, count, wanted, ctx, stats, keyed, part, latents, borrowed, pred_weight)
 
@@ -549,8 +615,10 @@
 def body(raw, starts, neg_owner, neg_block, enc_weight, tcn_weight, pred_weight):
     raw = raw[0]
     owners_count = lax.axis_size("tm") * lax.axis_size("stream")
-    rim_starts = jnp.zeros((2, 128), BF).at[0, 128 - HALO:].set(starts[0, -HALO:].astype(BF))
-    rim = shifted(jnp.concatenate([raw[:, -128:], rim_starts], axis=0), "tm", 1)
+    rim_starts = jnp.concatenate(
+        [jnp.zeros((1, 128 - HALO), BF), starts[:, -HALO:].astype(BF)], axis=1
+    )
+    rim = shifted(jnp.concatenate([raw[:, -128:], rim_starts, rim_starts], axis=0), "tm", 1)
     half_weight = (tcn_weight * 0.5).astype(BF)
     pack, push, slots, bd = prep(
         neg_owner.reshape(-1), neg_block.reshape(-1), raw, starts.reshape(-1, BLOCK), rim,
@@ -560,10 +628,11 @@
     latents, ctx, slopes, levels, rim_slopes, rim_levels, keyed = forward(
         pack, bd, half_weight, pred_weight
     )
-    wanted = pushed[:, PACK - 1, 64].astype(jnp.int32)
-    replies, order, count = answer(wanted, pack)
+    pushed, ctx = lax.optimization_barrier((pushed, ctx))
+    replies, order, count, wanted = answer(pushed, pack)
     answers = exchanged(replies)
     request_ctx = recompute(order, count, pushed, bd, half_weight)
+    answers, request_ctx = lax.optimization_barrier((answers, request_ctx))
     pred_grad, target_grad, stats = score(slots, answers, ctx, latents, levels, pred_weight, bd)
     got_stats = exchanged(stats)
     part, rim_grad = backward(

time: 342 us -> 240 us (0.70)
  the two profiles are of different devices: /device:TPU:88 before, /device:TPU:98 now
where the time goes in v2:
time: 240 us; the launch traced here: 235 us
  Pallas kernels  188 us (78%)
  starting transfers between devices  31.8 us (13%)
  local copies, waits for them, and re-layouts  7.5 us (3%)
  waiting for transfers between devices  6.67 us (3%)
    pallas_call x1, Pallas kernels, recompute(): pl.pallas_call(recompute_kernel, grid_spec=pltpu.PrefetchScalarGridSpec(n...  79.7 us
    pallas_call x1, Pallas kernels, score(): pl.pallas_call(score_kernel, grid_spec=pltpu.PrefetchScalarGridSpec(num_s...  29.4 us
    pallas_call x1, Pallas kernels, own(): pl.pallas_call(own_kernel, grid_spec=pltpu.PrefetchScalarGridSpec(num_sca...  29.1 us
    all_to_all x3, starting transfers between devices, exchanged(): lax.all_to_all(sent, ('tm', 'stream'), split_axis=0, concat_axis=0, tiled...  27.6 us
    pallas_call x1, Pallas kernels, forward(): pl.pallas_call(forward_kernel, grid=(steps,), out_shape=(jax.ShapeDtypeSt...  21.3 us
    pallas_call x1, Pallas kernels, backward(): pl.pallas_call(backward_kernel, grid=(steps,), out_shape=(jax.ShapeDtypeS...  16.1 us
    pallas_call x1, Pallas kernels, prep(): pl.pallas_call(prep_kernel, out_shape=(jax.ShapeDtypeStruct((blocks, PACK...  6.72 us
    unnamed x14, local copies, waits for them, and re-layouts  5.47 us
  transfers between devices with their start and end apart: 5, of which 3 were waited for; matrix products, arithmetic and copies ran while one was open for 2% of the time, Pallas kernels for 50%

profile of v2, /device:TPU:98, one launch (start us, length us, event | category | flops | bytes accessed | tf_op | source)
XLA Modules:
  0.0 235.4 jit_solution(2865595228361687881)
XLA Ops:
  0.0 0.7 slice_convert_fusion
  0.7 0.7 slice.9
  1.4 0.1 concatenate.6
  1.5 1.9 collective-permute-start
  3.4 0.8 copy.10
  4.2 0.7 reshape.27.owner_ref
  4.9 0.8 copy.11
  5.6 0.6 reshape.28.block_ref
  6.2 0.2 collective-permute-done.rim_ref
  6.4 0.6 copy-done.5
  7.0 6.7 %prep.1 = (bf16[32,32,128]{2,1,0:T(8,128)(2,1)}, bf16[256,32,128]{2,1,0:T(8,128)(2,1)}, s32[128]{0:T(128)}, bf16[128,1024]{1,0:T(8,128)(2,1)}) custom-call(s32[128]{0:T(128)} %reshape.27.owner_ref, s32[128]{0:T(128)} %reshape.28.block_ref, bf16[6,16384]{1,0:T(8,128)(2,1)} %bitcast.16, s32[32,128]{1,0:T(8,128)} %bitcast.18, bf16[8,128]{1,0:T(8,128)(2,1)} %copy-done.5, ...), custom_call_target="tpu_custom_call" | custom-call | tf_op jit(solution)/shard_map/prep/pallas_call | solution.py:123
  13.7 0.0 copy-start.1
  13.7 10.6 %all-to-all-start = ((bf16[128,2,32,128]{3,2,1,0:T(8,128)(2,1)}), bf16[128,2,32,128]{3,2,1,0:T(8,128)(2,1)S(1)}, u32[]{:S(2)}, u32[]{:S(2)}) async-start(bf16[128,2,32,128]{3,2,1,0:T(8,128)(2,1)} %bitcast.11), calls=%async_computation | async-start | bytes 4194304 | tf_op jit(solution)/shard_map/all_to_all | solution.py:611
  24.3 0.0 copy-done.1
  24.3 1.1 broadcast_multiply_fusion.w_ref
  25.4 21.3 %forward.1 = (bf16[4096,256]{1,0:T(8,128)(2,1)}, bf16[4096,256]{1,0:T(8,128)(2,1)}, bf16[4,4096,256]{2,1,0:T(8,128)(2,1)}, f32[4096,128]{1,0:T(8,128)}, bf16[4,3...) custom-call(bf16[32,32,128]{2,1,0:T(8,128)(2,1)} %get-tuple-element.30.pack_ref, ...), custom_call_target="tpu_custom_call" | custom-call | flops 5368709120 | bytes 18874368 | tf_op jit(solution)/shard_map/forward/pallas_call | solution.py:202
  46.7 4.6 %all-to-all-done = bf16[128,2,32,128]{3,2,1,0:T(8,128)(2,1)S(1)} async-done(((bf16[128,2,32,128]{3,2,1,0:T(8,128)(2,1)}), bf16[128,2,32,128]{3,2,1,0:T(8,128)(2,1)S(1)}, u32[]{:S(2)}, u32[]{:S(2)}) %all-to-all-start) | async-done | bytes 2097184 | tf_op jit(solution)/shard_map/all_to_all | solution.py:611
  51.2 1.3 copy-done
  52.6 5.4 %answer.1 = (bf16[256,32,128]{2,1,0:T(8,128)(2,1)}, s32[264]{0:T(512)}, s32[1]{0:T(128)}, s32[256]{0:T(256)}) custom-call(bf16[256,32,128]{2,1,0:T(8,128)(2,1)} %bitcast.9, bf16[32,32,128]{2,1,0:T(8,128)(2,1)} %get-tuple-element.30.pack_ref), custom_call_target="tpu_custom_call" | custom-call | tf_op jit(solution)/shard_map/answer/pallas_call | solution.py:264
  58.0 7.6 %all-to-all-start.1 = ((bf16[128,2,32,128]{3,2,1,0:T(8,128)(2,1)}), bf16[128,2,32,128]{3,2,1,0:T(8,128)(2,1)S(1)}, u32[]{:S(2)}, u32[]{:S(2)}) async-start(bf16[128,2,32,128]{3,2,1,0:T(8,128)(2,1)} %bitcast.13), calls=%async_computation.1 | async-start | bytes 4194304 | tf_op jit(solution)/shard_map/all_to_all | solution.py:611
  65.5 79.7 %recompute.1.ctx_ref = bf16[256,128,256]{2,1,0:T(8,128)(2,1)} custom-call(s32[264]{0:T(512)} %get-tuple-element.34.order_ref, s32[1]{0:T(128)} %get-tuple-element.35.count_ref, bf16[256,32,128]{2,1,0:T(8,128)(2,1)} %bitcast.10, bf16[128,1024]{1,0:T(8,128)(2,1)} %get-tuple-element.31.bd_ref, bf16[4,2,256,256]{3,2,1,0:T(8,128)(2,1)} %broadcast_multiply_fusion.w_ref), custom_call_target="tpu_custom_call" | custom-call | flops 53687091200 | bytes 20971520 | tf_op jit(solution)/shard_map/recompute/pallas_call | solution.py:349
  145.2 0.0 all-to-all-done.1
  145.2 1.3 copy-done.2
  146.6 29.4 %score.1 = (bf16[4096,256]{1,0:T(8,128)(2,1)}, f32[4096,256]{1,0:T(8,128)}, f32[256,2,128]{2,1,0:T(2,128)}) custom-call(s32[128]{0:T(128)} %get-tuple-element.39.slot_ref, bf16[256,32,128]{2,1,0:T(8,128)(2,1)} %bitcast.12, bf16[4096,256]{1,0:T(8,128)(2,1)} %get-tuple-element.41.ctx_ref, bf16[4096,256]{1,0:T(8,128)(2,1)} %get-tuple-element.42.lat_ref, ...), custom_call_target="tpu_custom_call" | custom-call | flops 5368709120 | bytes 16777216 | tf_op jit(solution)/shard_map/score/pallas_call | solution.py:436
  175.9 9.5 %all-to-all-start.2 = ((f32[128,2,2,128]{3,2,1,0:T(2,128)}), f32[128,2,2,128]{3,2,1,0:T(2,128)S(1)}, u32[]{:S(2)}, u32[]{:S(2)}) async-start(f32[128,2,2,128]{3,2,1,0:T(2,128)} %bitcast.17), calls=%async_computation.2 | async-start | bytes 524288 | tf_op jit(solution)/shard_map/all_to_all | solution.py:611
  185.4 16.1 %backward.1 = (f32[4096,256]{1,0:T(8,128)}, f32[32,256]{1,0:T(8,128)}) custom-call(bf16[4096,256]{1,0:T(8,128)(2,1)} %get-tuple-element.46.pred_grad_ref, bf16[4,4096,256]{2,1,0:T(8,128)(2,1)} %get-tuple-element.47.slope_ref, f32[4096,128]{1,0:T(8,128)} %get-tuple-element.43.level_ref, f32[4096,256]{1,0:T(8,128)} %get-tuple-element.48.target_grad_ref, ...), custom_call_target="tpu_custom_call" | custom-call | flops 4831838208 | bytes 23068672 | tf_op jit(solution)/shard_map/backward/pallas_call | solution.py:499
  201.5 2.2 collective-permute-start.1
  203.7 1.9 collective-permute-done.1.borrowed_ref
  205.6 0.0 all-to-all-done.2
  205.6 0.6 copy-done.4
  206.2 0.1 copy-done.3
  206.3 29.1 %own.1 = f32[4096,256]{1,0:T(8,128)} custom-call(s32[264]{0:T(512)} %get-tuple-element.34.order_ref, s32[1]{0:T(128)} %get-tuple-element.35.count_ref, s32[256]{0:T(256)} %get-tuple-element.36.wanted_ref, bf16[256,128,256]{2,1,0:T(8,128)(2,1)} %recompute.1.ctx_ref, f32[256,2,128]{2,1,0:T(2,128)} %bitcast.14, bf16[4096,256]{1,0:T(8,128)(2,1)} %get-tuple-element.45.keyed_ref, ...), custom_call_target="tpu_custom_call" | custom-call | tf_op jit(solution)/shard_map/own/pallas_call | solution.py:576
  (6 shorter events, 0.0 us)
Async XLA Ops:
  1.5 4.9 %collective-permute-start = (bf16[8,128]{1,0:T(8,128)(2,1)S(1)}, bf16[8,128]{1,0:T(8,128)(2,1)S(1)}, u32[]{:S(2)}, u32[]{:S(2)}) collective-permute-start(bf16[8,128]{1,0:T(8,128)(2,1)S(1)} %pad_maximum_fusion), channel_id=1, source_target_pairs={{0,4},{4,8},{8,12},{12,16},{16,20},{20,24},{24,28},{28,32},{32,36}... | collective-permute-start | bytes 6152 | tf_op jit(solution)/shard_map/ppermute | solution.py:605
  6.4 0.6 copy-start.5
  13.7 10.6 %copy-start.1 = (bf16[4,2,256,256]{3,2,1,0:T(8,128)(2,1)S(1)}, bf16[4,2,256,256]{3,2,1,0:T(8,128)(2,1)}, u32[]{:S(2)}) copy-start(bf16[4,2,256,256]{3,2,1,0:T(8,128)(2,1)} %w_ref.1) | copy-start | bytes 3145732
  13.7 37.5 %all-to-all-start = ((bf16[128,2,32,128]{3,2,1,0:T(8,128)(2,1)}), bf16[128,2,32,128]{3,2,1,0:T(8,128)(2,1)S(1)}, u32[]{:S(2)}, u32[]{:S(2)}) async-start(bf16[128,2,32,128]{3,2,1,0:T(8,128)(2,1)} %bitcast.11), calls=%async_computation | async-start | bytes 4194304 | tf_op jit(solution)/shard_map/all_to_all | solution.py:611
  51.2 1.3 copy-start
  58.0 87.3 %all-to-all-start.1 = ((bf16[128,2,32,128]{3,2,1,0:T(8,128)(2,1)}), bf16[128,2,32,128]{3,2,1,0:T(8,128)(2,1)S(1)}, u32[]{:S(2)}, u32[]{:S(2)}) async-start(bf16[128,2,32,128]{3,2,1,0:T(8,128)(2,1)} %bitcast.13), calls=%async_computation.1 | async-start | bytes 4194304 | tf_op jit(solution)/shard_map/all_to_all | solution.py:611
  145.2 1.3 copy-start.2
  175.9 29.7 %all-to-all-start.2 = ((f32[128,2,2,128]{3,2,1,0:T(2,128)}), f32[128,2,2,128]{3,2,1,0:T(2,128)S(1)}, u32[]{:S(2)}, u32[]{:S(2)}) async-start(f32[128,2,2,128]{3,2,1,0:T(2,128)} %bitcast.17), calls=%async_computation.2 | async-start | bytes 524288 | tf_op jit(solution)/shard_map/all_to_all | solution.py:611
  201.5 4.1 %collective-permute-start.1 = (f32[32,256]{1,0:T(8,128)}, f32[32,256]{1,0:T(8,128)S(1)}, u32[]{:S(2)}, u32[]{:S(2)}) collective-permute-start(f32[32,256]{1,0:T(8,128)} %get-tuple-element.52), channel_id=1, source_target_pairs={{4,0},{8,4},{12,8},{16,12},{20,16},{24,20},{28,24},{32,28},{36,32}... | collective-permute-start | bytes 98312 | tf_op jit(solution)/shard_map/ppermute | solution.py:605
  205.6 0.6 copy-start.4
  205.6 0.7 copy-start.3

commit v3 on v2

--- a/solution.py
+++ b/solution.py
@@ -13,6 +13,12 @@
 LAYERS = 4
 PACK = 32
 TOGETHER = 16
+PAIRED = 1
+PIECES = 4
+SKEW = 1
+GATHERED = 64
+CHUNK = 1024
+NOTE = 95
 LEAD = 20
 SEGMENT = 512
 SCORED = 4
@@ -40,8 +46,12 @@
     return half + half * jnp.tanh(half)
 
 
+def wide(x):
+    return jnp.concatenate([x, x], axis=1)
+
+
 def prep_kernel(owner_ref, block_ref, raw_ref, starts_ref, rim_ref, enc_ref,
-                pack_ref, push_ref, slot_ref, bd_ref, lines, packs, seen):
+                pack_ref, push_ref, slot_ref, bd_ref, lines, packs, turned, seen):
     blocks = pack_ref.shape[0]
     lines[...] = jnp.zeros_like(lines)
     for b in range(blocks):
@@ -79,36 +89,48 @@
     for b in range(blocks):
         packs[b, 30:31, :] = level[8 + b:9 + b]
         packs[b, 31:32, :] = level_halo[7 + b:8 + b]
-    pack_ref[...] = packs[...].astype(BF)
-
-    at = lax.broadcasted_iota(jnp.int32, (PACK, 128), 0)
+    quarter = lax.broadcasted_iota(jnp.int32, (PACK, 128), 1) >> 5
+    for group in range(blocks // 4):
+        four = [packs[group * 4 + q] for q in range(4)]
+        parts = []
+        for g in range(4):
+            part = four[g]
+            for q in range(4):
+                if q != g:
+                    part = jnp.where(quarter == q, pltpu.roll(four[q], (q - g) * 32 % 128, 1), part)
+            parts.append(part)
+        flipped = jnp.transpose(jnp.concatenate(parts, axis=0))
+        for q in range(4):
+            turned[group * 4 + q] = flipped[q * 32:(q + 1) * 32]
+    pack_ref[...] = turned[...].astype(BF)
+
     lane = lax.broadcasted_iota(jnp.int32, (PACK, 128), 1)
-    note = jnp.where((at == PACK - 1) & (lane >= 64), 1.0, 0.0)
+    note = jnp.where(lane == NOTE, 1.0, 0.0)
     unused = (-note).astype(BF)
 
     def clear(i, carry):
         push_ref[i] = unused
         return carry
 
-    lax.fori_loop(0, push_ref.shape[0], clear, 0)
+    lax.fori_loop(0, push_ref.shape[0], clear, 0, unroll=8)
 
     def forget(i, carry):
         seen[i] = 0
         return carry
 
-    lax.fori_loop(0, seen.shape[0], forget, 0)
+    lax.fori_loop(0, seen.shape[0], forget, 0, unroll=8)
 
     def send(i, carry):
-        owner = owner_ref[i]
+        owner = owner_ref[i % NEG, i // NEG]
         rank = seen[owner]
         seen[owner] = rank + 1
         slot = owner * CAP + rank
         slot_ref[i] = slot
-        wanted = block_ref[i].astype(F32)
-        push_ref[slot] = (packs[i // NEG] + note * wanted).astype(BF)
+        wanted = block_ref[i % NEG, i // NEG].astype(F32)
+        push_ref[slot] = (turned[i // NEG] + note * wanted).astype(BF)
         return carry
 
-    lax.fori_loop(0, blocks * NEG, send, 0)
+    lax.fori_loop(0, blocks * NEG, send, 0, unroll=4)
 
     bd_ref[...] = jnp.zeros_like(bd_ref)
     half_enc = (enc_ref[...].astype(F32) * 0.5).astype(BF)
@@ -133,6 +155,7 @@
         scratch_shapes=[
             pltpu.VMEM((blocks, 8, 512), F32),
             pltpu.VMEM((blocks, PACK, 128), F32),
+            pltpu.VMEM((blocks, PACK, 128), F32),
             pltpu.SMEM((owners_count,), jnp.int32),
         ],
         compiler_params=pltpu.CompilerParams(vmem_limit_bytes=VMEM),
@@ -140,18 +163,13 @@
     )(owners, wanted, raw, starts, rim, enc_weight)
 
 
-def turn(tiles):
-    return jnp.transpose(jnp.concatenate(tiles, axis=0).astype(F32))
-
-
-def encode_with_halo(turned, bd):
-    lane = lax.broadcasted_iota(jnp.int32, (HALO, 128), 1) & 31
-    halo = jnp.zeros((HALO, 128), F32)
-    for k in range(4):
-        moved = pltpu.roll(turned[k * 32:(k + 1) * 32], (6 * k - 24) % 128, 1)
-        halo = jnp.where((lane >= 6 * k) & (lane < 6 * k + 6), moved, halo)
-    rows = jnp.concatenate([turned, halo], axis=0).astype(BF)
-    return silu_of_half(dot(rows, bd))
+def halo_rows(pack):
+    lane = lax.broadcasted_iota(jnp.int32, (HALO, 128), 1)
+    halo = jnp.where(lane == 30, pltpu.roll(pack, 127, 1), 0.0)
+    for g in range(4):
+        moved = pltpu.roll(pack, (-26 * g - 24) % 128, 1)
+        halo = jnp.where((lane >= 6 * g) & (lane < 6 * g + 6), moved, halo)
+    return halo
 
 
 def layer_half(h, level, layer, w_ref):
@@ -163,13 +181,16 @@
 def forward_kernel(pack_ref, bd_ref, w_ref, pred_ref, lat_ref, ctx_ref, slope_ref, level_ref,
                    rim_slope_ref, rim_level_ref, keyed_ref):
     first = pl.program_id(0) == 0
-    turned = turn([pack_ref[q] for q in range(4)])
-    encoded = encode_with_halo(turned, bd_ref[...])
-    latent = jnp.concatenate(
-        [encoded[128:160, 0:256]] + [encoded[0:128, q * 256:(q + 1) * 256] for q in range(4)],
-        axis=0,
-    ).astype(BF)
-    columns = [turned[0:32, 31:32]] + [turned[:, q * 32 + 30:q * 32 + 31] for q in range(4)]
+    packs = pack_ref[...].reshape(4 * PACK, 128).astype(F32)
+    halo = halo_rows(packs[0:PACK])
+    rows = jnp.concatenate([packs, halo], axis=0)
+    encoded = silu_of_half(dot(rows.astype(BF), bd_ref[...]))
+    pieces, columns = [encoded[4 * PACK:, 0:256]], [halo[:, 30:31]]
+    for q in range(4):
+        for g in range(4):
+            pieces.append(encoded[q * PACK:(q + 1) * PACK, g * 256:(g + 1) * 256])
+            columns.append(packs[q * PACK:(q + 1) * PACK, g * 32 + 30:g * 32 + 31])
+    latent = jnp.concatenate(pieces, axis=0).astype(BF)
     level = jnp.broadcast_to(jnp.concatenate(columns, axis=0), (HALO + SEGMENT, 256))
     level_ref[...] = level[HALO:, 0:128]
     lat_ref[...] = latent[HALO:]
@@ -234,10 +255,17 @@
     )(pack, bd, half_weight, pred_weight)
 
 
-def answer_kernel(push_ref, pack_ref, answer_ref, order_ref, count_ref, wanted_ref, listed, arrived):
+def kept(count, half):
+    shared = ((count - half + 63) >> 6) << 5
+    return jnp.where(count > half, jnp.minimum(count, half + shared), count)
+
+
+def answer_kernel(push_ref, pack_ref, answer_ref, order_ref, bounds_ref, wanted_ref, extra_ref,
+                  listed, arrived):
     slots = push_ref.shape[0]
-    notes = push_ref[:, PACK - 16:, :].astype(F32)[:, 15, :]
-    listed[...] = jnp.transpose(notes)[64:72].astype(jnp.int32)
+    half = slots // 2
+    notes = push_ref[:, 0:16, :].astype(F32)[:, 0, :]
+    listed[...] = jnp.transpose(notes)[NOTE:NOTE + 1].astype(jnp.int32)
     pltpu.sync_copy(listed, arrived)
 
     def clear(i, carry):
@@ -254,7 +282,17 @@
         return count + jnp.where(wanted >= 0, 1, 0)
 
     count = lax.fori_loop(0, slots, reply, 0, unroll=8)
-    count_ref[0] = count
+    bounds_ref[0] = 0
+    bounds_ref[1] = kept(count, half)
+    bounds_ref[2] = count
+    extra_ref[...] = jnp.zeros_like(extra_ref)
+    extra_ref[half] = jnp.full((PACK, 128), count.astype(F32)).astype(BF)
+
+    def share(i, carry):
+        extra_ref[i - half] = push_ref[order_ref[i]]
+        return carry
+
+    lax.fori_loop(half, jnp.maximum(count, half), share, 0)
 
 
 def answer(pushed, pack):
@@ -266,94 +304,119 @@
         out_shape=(
             jax.ShapeDtypeStruct((slots, PACK, 128), BF),
             jax.ShapeDtypeStruct((slots + 8,), jnp.int32),
-            jax.ShapeDtypeStruct((1,), jnp.int32),
+            jax.ShapeDtypeStruct((3,), jnp.int32),
             jax.ShapeDtypeStruct((slots,), jnp.int32),
+            jax.ShapeDtypeStruct((slots // 2 + 1, PACK, 128), BF),
         ),
         in_specs=[vmem, vmem],
-        out_specs=(vmem, smem, smem, smem),
-        scratch_shapes=[pltpu.VMEM((8, slots), jnp.int32), pltpu.SMEM((8, slots), jnp.int32)],
+        out_specs=(vmem, smem, smem, smem, vmem),
+        scratch_shapes=[pltpu.VMEM((1, slots), jnp.int32), pltpu.SMEM((1, slots), jnp.int32)],
         compiler_params=pltpu.CompilerParams(vmem_limit_bytes=VMEM),
         name="answer",
     )(pushed, pack)
 
 
-def halo_rows(turned):
-    lane = lax.broadcasted_iota(jnp.int32, (HALO, 128), 1) & 31
-    halo = jnp.where(lane == 30, pltpu.roll(turned[0:HALO], 127, 1), 0.0)
-    for k in range(4):
-        moved = pltpu.roll(turned[k * 32:(k + 1) * 32], (6 * k - 24) % 128, 1)
-        halo = jnp.where((lane >= 6 * k) & (lane < 6 * k + 6), moved, halo)
-    return halo
-
-
-def recompute_kernel(order_ref, count_ref, push_ref, bd_ref, w_ref, ctx_ref,
-                     patches, level, here, there, left, right):
-    base = pl.program_id(0) * TOGETHER
+def request_stages(base, order_ref, push_ref, bd_ref, w_ref, ctx_ref, first_out,
+                   patches, level, here, there, left, right, gated, half_ref):
     times = LEAD + BLOCK - AHEAD
 
-    @pl.when(base < count_ref[0])
+    def pieces(first, parts=PIECES):
+        edges = [first + (times - first) * p // parts for p in range(parts + 1)]
+        return [(a * TOGETHER, b * TOGETHER) for a, b in zip(edges[:-1], edges[1:])]
+
+    def parts(a, b):
+        return [slice(c, min(c + 32, b)) for c in range(a, b, 32)]
+
+    for j in range(TOGETHER):
+        pack = push_ref[order_ref[base + j]].astype(F32)
+        patches[pl.ds(j, LEAD, stride=TOGETHER), :] = halo_rows(pack)[HALO - LEAD:]
+        for g in range(4):
+            count = min(32, BLOCK - AHEAD - g * 32)
+            own = pltpu.roll(pack, -32 * g % 128, 1) if g else pack
+            at = (LEAD + g * 32) * TOGETHER + j
+            patches[pl.ds(at, count, stride=TOGETHER), :] = own[:count]
+        if j % 4 == 3:
+            yield
+    enc = bd_ref[:, 0:256]
+    for a, b in pieces(0):
+        half_ref[a:b, :] = dot(patches[a:b, :].astype(BF), enc).astype(BF)
+        yield
+        level[a:b, :] = jnp.broadcast_to(patches[a:b, 30:31], (b - a, 128)).astype(BF)
+        for at in parts(a, b):
+            here[at, :] = silu_of_half(half_ref[at, :])
+        yield
+    source, target = here, there
+    first = 0
+    for layer in range(LAYERS):
+        first += 2**layer if layer else 2
+        back = 2**layer * TOGETHER
+        both = w_ref[layer].reshape(512, 256)
+        for a, b in pieces(first):
+            for at in parts(a, b):
+                gate = jnp.minimum(jnp.maximum(level[at, :] - float(layer), 0.0), 1.0)
+                gated[at, :] = source[at.start - back:at.stop - back, :] * wide(gate)
+            yield
+            x = jnp.concatenate([source[a:b, :], gated[a:b, :]], axis=1)
+            half_ref[a:b, :] = dot(x, both).astype(BF)
+            yield
+            for at in parts(a, b):
+                result = source[at, :] + silu_of_half(half_ref[at, :])
+                if layer < LAYERS - 1:
+                    target[at, :] = result
+                else:
+                    result = result.astype(F32)
+                    to = slice(at.start - first * TOGETHER, at.stop - first * TOGETHER)
+                    left[to, :] = result[:, 0:128]
+                    right[to, :] = result[:, 128:256]
+            yield
+        source, target = target, source
+    for j in range(TOGETHER):
+        rows = pl.ds(j, BLOCK, stride=TOGETHER)
+        ctx_ref[first_out + j] = jnp.concatenate([left[rows, :], right[rows, :]], axis=1).astype(BF)
+        if j % 4 == 3:
+            yield
+
+
+def recompute_kernel(order_ref, bounds_ref, push_ref, bd_ref, w_ref, ctx_ref, *scratch):
+    base = bounds_ref[0] + pl.program_id(0) * PAIRED * TOGETHER
+
+    @pl.when(base < bounds_ref[1])
     def _():
-        for part in range(TOGETHER // 4):
-            turned = turn([push_ref[order_ref[base + part * 4 + q]] for q in range(4)])
-            halo = halo_rows(turned)
-            for q in range(4):
-                j = part * 4 + q
-                shift = (-32 * q) % 128
-                own = pltpu.roll(turned, shift, 1) if q else turned
-                before = pltpu.roll(halo, shift, 1) if q else halo
-                patches[pl.ds(j, LEAD, stride=TOGETHER), :] = before[HALO - LEAD:]
-                patches[pl.ds(LEAD * TOGETHER + j, BLOCK - AHEAD, stride=TOGETHER), :] = own[:BLOCK - AHEAD]
-        enc = bd_ref[:, 0:256]
-        row = lax.broadcasted_iota(jnp.int32, (128, 128), 0)
-        pick = jnp.where(row == 30, 1.0, 0.0).astype(BF)
-
-        def pieces(first, parts):
-            edges = [first + (times - first) * p // parts for p in range(parts + 1)]
-            return [(a * TOGETHER, b * TOGETHER) for a, b in zip(edges[:-1], edges[1:])]
-
-        for a, b in pieces(0, 4):
-            x = patches[a:b, :].astype(BF)
-            here[a:b, :] = silu_of_half(dot(x, enc)).astype(BF)
-            level[a:b, :] = dot(x, pick).astype(BF)
-        source, target = here, there
-        first = 0
-        for layer in range(LAYERS):
-            first += 2**layer if layer else 2
-            back = 2**layer * TOGETHER
-            for a, b in pieces(first, 4):
-                h = source[a:b, :]
-                gate = jnp.minimum(jnp.maximum(level[a:b, :] - float(layer), 0.0), 1.0)
-                gated = source[a - back:b - back, :] * jnp.concatenate([gate, gate], axis=1)
-                half = dot(h, w_ref[layer, 0]) + dot(gated, w_ref[layer, 1])
-                result = h.astype(F32) + silu_of_half(half)
-                if layer < LAYERS - 1:
-                    target[a:b, :] = result.astype(BF)
-                else:
-                    at = first * TOGETHER
-                    left[a - at:b - at, :] = result[:, 0:128]
-                    right[a - at:b - at, :] = result[:, 128:256]
-            source, target = target, source
-        for j in range(TOGETHER):
-            rows = pl.ds(j, BLOCK, stride=TOGETHER)
-            ctx_ref[j] = jnp.concatenate([left[rows, :], right[rows, :]], axis=1).astype(BF)
-
-
-def last_step(count_ref):
-    return jnp.maximum(count_ref[0] - 1, 0) // TOGETHER
-
-
-def recompute(order, count, pushed, bd, half_weight):
-    slots = pushed.shape[0]
+        each = len(scratch) // PAIRED
+        waiting = [
+            request_stages(
+                base + p * TOGETHER, order_ref, push_ref, bd_ref, w_ref, ctx_ref, p * TOGETHER,
+                *scratch[p * each:(p + 1) * each],
+            )
+            for p in range(PAIRED)
+        ]
+        for p, stages in enumerate(waiting):
+            for _ in range(SKEW * (PAIRED - 1 - p)):
+                next(stages)
+        while waiting:
+            waiting = [stages for stages in waiting if next(stages, True) is None]
+
+
+def last_step(count, together):
+    return jnp.maximum(count - 1, 0) // together
+
+
+def recompute(order, bounds, pushed, bd, half_weight):
+    slots = order.shape[0] // TOGETHER * TOGETHER
+    together = PAIRED * TOGETHER
     times = LEAD + BLOCK - AHEAD
     whole = lambda *shape: pl.BlockSpec(shape, lambda i, o, c: (0,) * len(shape))
     return pl.pallas_call(
         recompute_kernel,
         grid_spec=pltpu.PrefetchScalarGridSpec(
             num_scalar_prefetch=2,
-            grid=(slots // TOGETHER,),
-            in_specs=[whole(slots, PACK, 128), whole(128, 1024), whole(LAYERS, 2, 256, 256)],
+            grid=(slots // TOGETHER // PAIRED,),
+            in_specs=[whole(*pushed.shape), whole(128, 1024), whole(LAYERS, 2, 256, 256)],
             out_specs=pl.BlockSpec(
-                (TOGETHER, BLOCK, 256), lambda i, o, c: (jnp.minimum(i, last_step(c)), 0, 0)
+                (together, BLOCK, 256),
+                lambda i, o, c: (
+                    jnp.minimum(c[0] // together + i, last_step(c[1], together)), 0, 0
+                ),
             ),
             scratch_shapes=[
                 pltpu.VMEM((times * TOGETHER, 128), F32),
@@ -362,7 +425,9 @@
                 pltpu.VMEM((times * TOGETHER, 256), BF),
                 pltpu.VMEM((BLOCK * TOGETHER, 128), F32),
                 pltpu.VMEM((BLOCK * TOGETHER, 128), F32),
-            ],
+                pltpu.VMEM((times * TOGETHER, 256), BF),
+                pltpu.VMEM((times * TOGETHER, 256), BF),
+            ] * PAIRED,
         ),
         out_shape=jax.ShapeDtypeStruct((slots, BLOCK, 256), BF),
         compiler_params=pltpu.CompilerParams(vmem_limit_bytes=VMEM),
@@ -371,11 +436,7 @@
             transcendentals=slots * 160 * 256 * 5,
         ),
         name="recompute",
-    )(order, count, pushed, bd, half_weight)
-
-
-def square_sums(x):
-    return dot((x * x).astype(BF), jnp.ones((256, 128), BF))
+    )(order, bounds, pushed, bd, half_weight)
 
 
 def score_kernel(slot_ref, answer_ref, ctx_ref, lat_ref, level_ref, pred_ref, bd_ref,
@@ -386,46 +447,56 @@
     def _():
         stats_ref[...] = jnp.zeros_like(stats_ref)
 
+    blocks = range(SCORED)
     slots = [slot_ref[step * SCORED * NEG + i] for i in range(SCORED * NEG)]
     lane = lax.broadcasted_iota(jnp.int32, (BLOCK, 128), 1)
-    raw_preds = dot(ctx_ref[...], pred_ref[...])
-    for g in range(SCORED):
-        at = slice(g * BLOCK, (g + 1) * BLOCK)
-        raw_pred = raw_preds[at]
-        pred_scale = lax.rsqrt(row_sum(raw_pred * raw_pred) + EPSILON)
-        unit = raw_pred * pred_scale
-        query = unit.astype(BF)
-        query_f = query.astype(F32)
-
-        turned = turn([answer_ref[slots[g * NEG + j]] for j in range(NEG)])
-        encoded = silu_of_half(dot(turned.astype(BF), bd_ref[...]))
-        keys = []
-        for j in range(NEG):
-            negative = encoded[:, j * 256:(j + 1) * 256]
-            key_scale = lax.rsqrt(square_sums(negative) + EPSILON)
-            keys.append((negative * jnp.concatenate([key_scale, key_scale], axis=1)).astype(BF))
-        keys = jnp.concatenate(keys, axis=0)
-
+    ats = [slice(g * BLOCK, (g + 1) * BLOCK) for g in blocks]
+    packs = [
+        jnp.concatenate([answer_ref[slots[g * NEG + j]] for j in range(NEG)], axis=0) for g in blocks
+    ]
+    raw_pred = [dot(ctx_ref[at, :], pred_ref[...]) for at in ats]
+    half = [dot(pack, bd_ref[...]) for pack in packs]
+    pred_scale = [lax.rsqrt(row_sum(x * x) + EPSILON) for x in raw_pred]
+    unit = [x * y for x, y in zip(raw_pred, pred_scale)]
+    query = [x.astype(BF) for x in unit]
+    keys = []
+    for g in blocks:
+        pieces = []
+        for j in range(4):
+            negative = silu_of_half(half[g][:, j * 256:(j + 1) * 256])
+            key_scale = lax.rsqrt(row_sum(negative * negative) + EPSILON)
+            pieces.append((negative * (key_scale)).astype(BF))
+        keys.append(jnp.concatenate(pieces, axis=0))
+    scores = [dot_nt(query[g], keys[g]) for g in blocks]
+    exp_neg = [jnp.exp(SCALE * x) for x in scores]
+    both = [dot(exp_neg[g].astype(BF), keys[g]) for g in blocks]
+    sums = [row_sum(x) for x in exp_neg]
+    columns = jnp.zeros((BLOCK, 128), F32)
+    for g in blocks:
+        at = ats[g]
+        query_f = query[g].astype(F32)
         latent = lat_ref[at, :].astype(F32)
         usable = jnp.where(level_ref[at, 0:1] > 2.0, 1.0, 0.0)
         own_scale = lax.rsqrt(row_sum(latent * latent) + EPSILON)
         positive = SCALE * row_sum(query_f * latent) * own_scale
-        exp_neg = jnp.exp(SCALE * dot_nt(query, keys))
         exp_pos = jnp.exp(positive)
-        share = usable / (exp_pos + row_sum(exp_neg))
+        share = usable / (exp_pos + sums[g])
         d_pos = share * exp_pos - usable
-        query_grad = SCALE * (
-            dot((exp_neg * share).astype(BF), keys) + (d_pos * own_scale) * latent
+        pull = SCALE * d_pos * own_scale
+        query_grad = (SCALE * share) * both[g] + (pull) * latent
+        target_grad_ref[at, :] = (
+            (pull) * query_f - (d_pos * positive * own_scale * own_scale) * latent
         )
-        target_grad_ref[at, :] = (SCALE * d_pos * own_scale) * query_f - (
-            d_pos * positive * own_scale * own_scale
-        ) * latent
-        along = row_sum(unit * query_grad)
-        pred_grad_ref[at, :] = (pred_scale * (query_grad - along * unit)).astype(BF)
-        columns = jnp.where(lane == 0, pred_scale, jnp.where(lane == 1, share, 0.0))
-        rows = jnp.transpose(columns)[0:2]
-        for j in range(NEG):
-            stats_ref[slots[g * NEG + j]] = rows
+        along = row_sum(unit[g] * query_grad)
+        pred_grad_ref[at, :] = (
+            (pred_scale[g]) * (query_grad - (along) * unit[g])
+        ).astype(BF)
+        columns = jnp.where(lane == 2 * g, pred_scale[g], columns)
+        columns = jnp.where(lane == 2 * g + 1, share, columns)
+    rows = jnp.transpose(columns)
+    for i in range(SCORED * NEG):
+        g = i // NEG
+        stats_ref[slots[i]] = rows[2 * g:2 * g + 2]
 
 
 def score(slots, answers, ctx, latents, levels, pred_weight, bd):
@@ -474,20 +545,22 @@
             gated = jnp.where(level > layer, back, 0.0)
             cotangent = (
                 cotangent
-                + dot_nt(back.astype(BF), w_ref[layer, 0])
-                + dot_nt(earlier(gated, 2**layer, layer).astype(BF), w_ref[layer, 1])
+                + dot(
+                    jnp.concatenate([back, earlier(gated, 2**layer, layer)], axis=1).astype(BF),
+                    w_ref[layer].reshape(512, 256),
+                )
             )
         return cotangent
 
-    context_rows = dot_nt(pred_grad_ref[...], pred_ref[...])
+    context_rows = dot(pred_grad_ref[...], pred_ref[...])
     cotangent = earlier(context_rows, AHEAD, LAYERS)
-    level = jnp.broadcast_to(level_ref[:, 0:1], (SEGMENT, 256))
+    level = wide(level_ref[...])
     out_ref[...] = through_layers(cotangent, slope_ref, level) + target_grad_ref[...]
 
     @pl.when(pl.program_id(0) == pl.num_programs(0) - 1)
     def _():
         cotangent = earlier(jnp.zeros((HALO, 256), F32), AHEAD, LAYERS)
-        level = jnp.broadcast_to(rim_level_ref[:, 0:1], (HALO, 256))
+        level = wide(rim_level_ref[...])
         rim_ref[...] = through_layers(cotangent, rim_slope_ref, level)
 
 
@@ -523,65 +596,75 @@
     )(pred_grad, slopes, levels, target_grad, rim_slopes, rim_levels, pred_weight, weight)
 
 
-def own_kernel(order_ref, count_ref, wanted_ref, ctx_ref, stats_ref, keyed_ref, part_ref, lat_ref,
+def own_kernel(order_ref, bounds_ref, wanted_ref, ctx_ref, help_ref, stats_ref, keyed_ref, part_ref, lat_ref,
                borrowed_ref, pred_ref, out_ref, total):
     step = pl.program_id(0)
-    request_steps = pl.num_programs(0) - total.shape[0] // SEGMENT
+    request_steps = pl.num_programs(0) - total.shape[0] // CHUNK
 
     @pl.when(step == 0)
     def _():
         total[...] = jnp.zeros_like(total)
 
-    @pl.when((step < request_steps) & (step * TOGETHER < count_ref[0]))
+    @pl.when((step < request_steps) & (step * GATHERED < bounds_ref[2]))
     def _():
-        for part in range(0, TOGETHER, 4):
+        for part in range(0, GATHERED, 4):
             found = []
             for j in range(part, part + 4):
-                at = step * TOGETHER + j
+                at = step * GATHERED + j
                 slot = order_ref[at]
                 block = wanted_ref[slot]
                 rows = pl.ds(pl.multiple_of(block * BLOCK, BLOCK), BLOCK)
                 stats = stats_ref[slot]
+                helped = jnp.where(at < bounds_ref[2], help_ref[j], jnp.zeros((BLOCK, 256), BF))
+                ctx = jnp.where(at < bounds_ref[1], ctx_ref[j], helped)
                 pred_scale, share = stats[0:1], stats[1:2]
-                scores = dot_nt(keyed_ref[rows, :], ctx_ref[j]) * (SCALE * pred_scale)
+                scores = dot_nt(keyed_ref[rows, :], ctx) * (SCALE * pred_scale)
                 weighted = jnp.exp(scores) * (share * pred_scale)
-                weighted = jnp.where(at < count_ref[0], weighted, 0.0)
-                found.append((rows, dot(weighted.astype(BF), ctx_ref[j])))
+                weighted = jnp.where(at < bounds_ref[2], weighted, 0.0)
+                found.append((rows, dot(weighted.astype(BF), ctx)))
             for rows, addend in found:
                 total[rows, :] += addend
 
     @pl.when(step >= request_steps)
     def _():
         chunk = step - request_steps
-        rows = pl.ds(pl.multiple_of(chunk * SEGMENT, SEGMENT), SEGMENT)
+        rows = pl.ds(pl.multiple_of(chunk * CHUNK, CHUNK), CHUNK)
         direct = SCALE * dot(total[rows, :].astype(BF), pred_ref[...])
         latent = lat_ref[...].astype(F32)
         key_scale = lax.rsqrt(row_sum(latent * latent) + EPSILON)
         key = latent * key_scale
-        out_ref[...] = part_ref[...] + key_scale * (direct - row_sum(key * direct) * key)
+        along = row_sum(key * direct)
+        out_ref[...] = part_ref[...] + key_scale * (direct - along * key)
 
         @pl.when(step == pl.num_programs(0) - 1)
         def _():
-            out_ref[SEGMENT - HALO:, :] += borrowed_ref[...]
-
-
-def own(order, count, wanted, ctx, stats, keyed, part, latents, borrowed, pred_weight):
+            out_ref[CHUNK - HALO:, :] += borrowed_ref[...]
+
+
+def own(order, bounds, wanted, ctx, helped, stats, keyed, part, latents, borrowed, pred_weight):
     rows = part.shape[0]
     slots = ctx.shape[0]
-    request_steps = slots // TOGETHER
+    request_steps = slots // GATHERED
+    first_help = slots // 2 // GATHERED
     whole = lambda *shape: pl.BlockSpec(shape, lambda i, o, c, w: (0,) * len(shape))
     chunk_of = pl.BlockSpec(
-        (SEGMENT, 256), lambda i, o, c, w: (jnp.maximum(i - request_steps, 0), 0)
+        (CHUNK, 256), lambda i, o, c, w: (jnp.maximum(i - request_steps, 0), 0)
     )
     return pl.pallas_call(
         own_kernel,
         grid_spec=pltpu.PrefetchScalarGridSpec(
             num_scalar_prefetch=3,
-            grid=(request_steps + rows // SEGMENT,),
+            grid=(request_steps + rows // CHUNK,),
             in_specs=[
                 pl.BlockSpec(
-                    (TOGETHER, BLOCK, 256),
-                    lambda i, o, c, w: (jnp.minimum(i, last_step(c)), 0, 0),
+                    (GATHERED, BLOCK, 256),
+                    lambda i, o, c, w: (jnp.minimum(i, last_step(c[1], GATHERED)), 0, 0),
+                ),
+                pl.BlockSpec(
+                    (GATHERED, BLOCK, 256),
+                    lambda i, o, c, w: (
+                        jnp.clip(i - first_help, 0, last_step(c[2] - slots // 2, GATHERED)), 0, 0
+                    ),
                 ),
                 whole(slots, 2, 128),
                 whole(rows, 256),
@@ -596,13 +679,17 @@
         out_shape=jax.ShapeDtypeStruct((rows, 256), F32),
         compiler_params=pltpu.CompilerParams(vmem_limit_bytes=VMEM),
         name="own",
-    )(order, count, wanted, ctx, stats, keyed, part, latents, borrowed, pred_weight)
+    )(order, bounds, wanted, ctx, helped, stats, keyed, part, latents, borrowed, pred_weight)
 
 
 def shifted(block, axis, distance):
     devices = range(lax.axis_size(axis))
     route = [(i - distance, i) for i in devices if i - distance in devices]
     return lax.ppermute(block, axis, route)
+
+
+def swapped(block, axis):
+    return lax.ppermute(block, axis, [(i, i ^ 1) for i in range(lax.axis_size(axis))])
 
 
 def exchanged(slots):
@@ -620,8 +707,10 @@
     )
     rim = shifted(jnp.concatenate([raw[:, -128:], rim_starts, rim_starts], axis=0), "tm", 1)
     half_weight = (tcn_weight * 0.5).astype(BF)
+    tcn_back = jnp.swapaxes(tcn_weight, 2, 3)
+    pred_back = pred_weight.T
     pack, push, slots, bd = prep(
-        neg_owner.reshape(-1), neg_block.reshape(-1), raw, starts.reshape(-1, BLOCK), rim,
+        neg_owner[0].T, neg_block[0].T, raw, starts.reshape(-1, BLOCK), rim,
         enc_weight, owners_count,
     )
     pushed = exchanged(push)
@@ -629,18 +718,28 @@
         pack, bd, half_weight, pred_weight
     )
     pushed, ctx = lax.optimization_barrier((pushed, ctx))
-    replies, order, count, wanted = answer(pushed, pack)
+    replies, order, bounds, wanted, extra = answer(pushed, pack)
     answers = exchanged(replies)
-    request_ctx = recompute(order, count, pushed, bd, half_weight)
+    half = order.shape[0] // TOGETHER * TOGETHER // 2
+    shared = swapped(extra, "tm")
+    request_ctx = recompute(order, bounds, pushed, bd, half_weight)
+    mate_count = shared[half, 0, 0].astype(jnp.int32)
+    mate_bounds = jnp.stack([kept(mate_count, half) - half, mate_count - half])
+    helped = swapped(
+        recompute(
+            lax.iota(jnp.int32, half), jnp.maximum(mate_bounds, 0), shared, bd, half_weight
+        ),
+        "tm",
+    )
     answers, request_ctx = lax.optimization_barrier((answers, request_ctx))
     pred_grad, target_grad, stats = score(slots, answers, ctx, latents, levels, pred_weight, bd)
     got_stats = exchanged(stats)
     part, rim_grad = backward(
-        pred_grad, slopes, levels, target_grad, rim_slopes, rim_levels, pred_weight, tcn_weight
+        pred_grad, slopes, levels, target_grad, rim_slopes, rim_levels, pred_back, tcn_back
     )
     borrowed = shifted(rim_grad, "tm", -1)
     return own(
-        order, count, wanted, request_ctx, got_stats, keyed, part, latents, borrowed, pred_weight
+        order, bounds, wanted, request_ctx, helped, got_stats, keyed, part, latents, borrowed, pred_weight
     )[None]
 
 

time: 240 us -> 220 us (0.917)
  the two profiles are of different devices: /device:TPU:98 before, /device:TPU:15 now
where the time goes in v3:
time: 220 us
  Pallas kernels  144 us (65%)
  starting transfers between devices  50 us (23%)
  waiting for transfers between devices  14.5 us (7%)
  local copies, waits for them, and re-layouts  7.79 us (4%)
  other arithmetic  2.42 us (1%)
    pallas_call x2, Pallas kernels, recompute(): pl.pallas_call(recompute_kernel, grid_spec=pltpu.PrefetchScalarGridSpec(n...  54.4 us
    all_to_all x3, starting transfers between devices, exchanged(): lax.all_to_all(sent, ('tm', 'stream'), split_axis=0, concat_axis=0, tiled...  27.9 us
    pallas_call x1, Pallas kernels, own(): pl.pallas_call(own_kernel, grid_spec=pltpu.PrefetchScalarGridSpec(num_sca...  21.5 us
    pallas_call x1, Pallas kernels, score(): pl.pallas_call(score_kernel, grid_spec=pltpu.PrefetchScalarGridSpec(num_s...  20.5 us
    pallas_call x1, Pallas kernels, forward(): pl.pallas_call(forward_kernel, grid=(steps,), out_shape=(jax.ShapeDtypeSt...  20.4 us
    ppermute x2, starting transfers between devices, swapped(): lax.ppermute(block, axis, [(i, i ^ 1) for i in range(lax.axis_size(axis))])  16.2 us
    pallas_call x1, Pallas kernels, backward(): pl.pallas_call(backward_kernel, grid=(steps,), out_shape=(jax.ShapeDtypeS...  15.9 us
    pallas_call x1, Pallas kernels, answer(): pl.pallas_call(answer_kernel, out_shape=(jax.ShapeDtypeStruct((slots, PAC...  6.25 us
  transfers between devices with their start and end apart: 7, of which 4 were waited for; matrix products, arithmetic and copies ran while one was open for 1% of the time, Pallas kernels for 49%

profile of v3, /device:TPU:15, one launch (start us, length us, event | category | flops | bytes accessed | tf_op | source)
XLA Modules:
  0.0 219.8 jit_solution(12435700233614584254)
XLA Ops:
  0.0 0.7 slice.13
  0.7 0.7 slice_convert_fusion
  1.5 3.7 %collective-permute-start = (bf16[8,128]{1,0:T(8,128)(2,1)S(1)}, bf16[8,128]{1,0:T(8,128)(2,1)S(1)}, u32[]{:S(2)}, u32[]{:S(2)}) collective-permute-start(bf16[8,128]{1,0:T(8,128)(2,1)S(1)} %pad_maximum_fusion), channel_id=1, source_target_pairs={{0,4},{4,8},{8,12},{12,16},{16,20},{20,24},{24,28},{28,32},{32,36}... | collective-permute-start | bytes 6152 | tf_op jit(solution)/shard_map/ppermute | solution.py:688
  5.2 0.7 collective-permute-done.rim_ref
  5.9 0.5 copy-done.6
  6.4 5.4 %prep.1 = (bf16[32,32,128]{2,1,0:T(8,128)(2,1)}, bf16[256,32,128]{2,1,0:T(8,128)(2,1)}, s32[128]{0:T(128)}, bf16[128,1024]{1,0:T(8,128)(2,1)}) custom-call(s32[4,32]{1,0:T(4,128)} %bitcast.32, s32[4,32]{1,0:T(4,128)} %bitcast.33, bf16[6,16384]{1,0:T(8,128)(2,1)} %bitcast.29, s32[32,128]{1,0:T(8,128)} %bitcast.31, bf16[8,128]{1,0:T(8,128)(2,1)} %copy-done.6, ...), custom_call_target="tpu_custom_call" | custom-call | tf_op jit(solution)/shard_map/prep/pallas_call | solution.py:145
  11.9 11.2 %all-to-all-start = ((bf16[128,2,32,128]{3,2,1,0:T(8,128)(2,1)}), bf16[128,2,32,128]{3,2,1,0:T(8,128)(2,1)S(1)}, u32[]{:S(2)}, u32[]{:S(2)}) async-start(bf16[128,2,32,128]{3,2,1,0:T(8,128)(2,1)} %bitcast.25), calls=%async_computation | async-start | bytes 4194304 | tf_op jit(solution)/shard_map/all_to_all | solution.py:698
  23.1 1.1 broadcast_multiply_fusion.w_ref
  24.1 20.4 %forward.1 = (bf16[4096,256]{1,0:T(8,128)(2,1)}, bf16[4096,256]{1,0:T(8,128)(2,1)}, bf16[4,4096,256]{2,1,0:T(8,128)(2,1)}, f32[4096,128]{1,0:T(8,128)}, bf16[4,3...) custom-call(bf16[32,32,128]{2,1,0:T(8,128)(2,1)} %get-tuple-element.31.pack_ref, ...), custom_call_target="tpu_custom_call" | custom-call | flops 5368709120 | bytes 18874368 | tf_op jit(solution)/shard_map/forward/pallas_call | solution.py:223
  44.5 5.6 %all-to-all-done = bf16[128,2,32,128]{3,2,1,0:T(8,128)(2,1)S(1)} async-done(((bf16[128,2,32,128]{3,2,1,0:T(8,128)(2,1)}), bf16[128,2,32,128]{3,2,1,0:T(8,128)(2,1)S(1)}, u32[]{:S(2)}, u32[]{:S(2)}) %all-to-all-start) | async-done | bytes 2097184 | tf_op jit(solution)/shard_map/all_to_all | solution.py:698
  50.1 1.3 copy-done
  51.4 6.3 %answer.1 = (bf16[256,32,128]{2,1,0:T(8,128)(2,1)}, s32[264]{0:T(512)}, s32[3]{0:T(128)}, s32[256]{0:T(256)}, bf16[129,32,128]{2,1,0:T(8,128)(2,1)}) custom-call(bf16[256,32,128]{2,1,0:T(8,128)(2,1)} %bitcast.21, bf16[32,32,128]{2,1,0:T(8,128)(2,1)} %get-tuple-element.31.pack_ref), custom_call_target="tpu_custom_call" | custom-call | tf_op jit(solution)/shard_map/answer/pallas_call | solution.py:302
  57.7 0.1 collective-permute-start.1
  57.8 2.9 %collective-permute-done.1.push_ref = bf16[129,32,128]{2,1,0:T(8,128)(2,1)S(1)} collective-permute-done((bf16[129,32,128]{2,1,0:T(8,128)(2,1)}, bf16[129,32,128]{2,1,0:T(8,128)(2,1)S(1)}, u32[]{:S(2)}, u32[]{:S(2)}) %collective-permute-start.1) | collective-permute-done | bytes 1056800 | tf_op jit(solution)/shard_map/ppermute | solution.py:692
  60.7 0.6 slice.15
  61.9 0.6 add_maximum_fusion.bounds_ref
  62.5 0.5 iota.3.order_ref
  63.0 3.4 %recompute.3 = bf16[128,128,256]{2,1,0:T(8,128)(2,1)} custom-call(s32[128]{0:T(128)} %iota.3.order_ref, s32[2]{0:T(128)} %add_maximum_fusion.bounds_ref, bf16[129,32,128]{2,1,0:T(8,128)(2,1)} %copy-done.7, bf16[128,1024]{1,0:T(8,128)(2,1)} %get-tuple-element.32.bd_ref, bf16[4,2,256,256]{3,2,1,0:T(8,128)(2,1)} %broadcast_multiply_fusion.w_ref), custom_call_target="tpu_custom_call" | custom-call | flops 26843545600 | bytes 20971520 | tf_op jit(solution)/shard_map/recompute/pallas_call | solution.py:409
  66.4 16.1 %collective-permute-start.2 = (bf16[128,128,256]{2,1,0:T(8,128)(2,1)}, bf16[128,128,256]{2,1,0:T(8,128)(2,1)}, u32[]{:S(2)}, u32[]{:S(2)}) collective-permute-start(bf16[128,128,256]{2,1,0:T(8,128)(2,1)} %recompute.3), channel_id=1, source_target_pairs={{0,4},{4,0},{8,12},{12,8},{16,20},{20,16},{24,28},{28,24},{32,36},... | collective-permute-start | bytes 25165832 | tf_op jit(solution)/shard_map/ppermute | solution.py:692
  82.5 1.3 copy.9
  83.8 0.7 copy.8
  84.6 7.2 %all-to-all-start.1 = ((bf16[128,2,32,128]{3,2,1,0:T(8,128)(2,1)}), bf16[128,2,32,128]{3,2,1,0:T(8,128)(2,1)S(1)}, u32[]{:S(2)}, u32[]{:S(2)}) async-start(bf16[128,2,32,128]{3,2,1,0:T(8,128)(2,1)} %bitcast.8), calls=%async_computation.1 | async-start | bytes 4194304 | tf_op jit(solution)/shard_map/all_to_all | solution.py:698
  91.7 51.1 %recompute.2.ctx_ref = bf16[256,128,256]{2,1,0:T(8,128)(2,1)} custom-call(s32[264]{0:T(512)} %get-tuple-element.35.order_ref, s32[3]{0:T(128)} %get-tuple-element.36.bounds_ref, bf16[256,32,128]{2,1,0:T(8,128)(2,1)} %bitcast.22, bf16[128,1024]{1,0:T(8,128)(2,1)} %get-tuple-element.32.bd_ref, bf16[4,2,256,256]{3,2,1,0:T(8,128)(2,1)} %broadcast_multiply_fusion.w_ref), custom_call_target="tpu_custom_call" | custom-call | flops 53687091200 | bytes 20971520 | tf_op jit(solution)/shard_map/recompute/pallas_call | solution.py:409
  142.8 1.3 copy-done.2
  144.1 20.5 %score.1 = (bf16[4096,256]{1,0:T(8,128)(2,1)}, f32[4096,256]{1,0:T(8,128)}, f32[256,2,128]{2,1,0:T(2,128)}) custom-call(s32[128]{0:T(128)} %get-tuple-element.41.slot_ref, bf16[256,32,128]{2,1,0:T(8,128)(2,1)} %bitcast.24, bf16[4096,256]{1,0:T(8,128)(2,1)} %get-tuple-element.43.ctx_ref, bf16[4096,256]{1,0:T(8,128)(2,1)} %get-tuple-element.44.lat_ref, ...), custom_call_target="tpu_custom_call" | custom-call | flops 5368709120 | bytes 16777216 | tf_op jit(solution)/shard_map/score/pallas_call | solution.py:507
  164.6 9.5 %all-to-all-start.2 = ((f32[128,2,2,128]{3,2,1,0:T(2,128)}), f32[128,2,2,128]{3,2,1,0:T(2,128)S(1)}, u32[]{:S(2)}, u32[]{:S(2)}) async-start(f32[128,2,2,128]{3,2,1,0:T(2,128)} %bitcast.30), calls=%async_computation.2 | async-start | bytes 524288 | tf_op jit(solution)/shard_map/all_to_all | solution.py:698
  174.1 15.9 %backward.1 = (f32[4096,256]{1,0:T(8,128)}, f32[32,256]{1,0:T(8,128)}) custom-call(bf16[4096,256]{1,0:T(8,128)(2,1)} %get-tuple-element.48.pred_grad_ref, bf16[4,4096,256]{2,1,0:T(8,128)(2,1)} %get-tuple-element.49.slope_ref, f32[4096,128]{1,0:T(8,128)} %get-tuple-element.45.level_ref, f32[4096,256]{1,0:T(8,128)} %get-tuple-element.50.target_grad_ref, ...), custom_call_target="tpu_custom_call" | custom-call | flops 4831838208 | bytes 23068672 | tf_op jit(solution)/shard_map/backward/pallas_call | solution.py:572
  190.0 2.3 %collective-permute-start.3 = (f32[32,256]{1,0:T(8,128)}, f32[32,256]{1,0:T(8,128)S(1)}, u32[]{:S(2)}, u32[]{:S(2)}) collective-permute-start(f32[32,256]{1,0:T(8,128)} %get-tuple-element.54), channel_id=1, source_target_pairs={{4,0},{8,4},{12,8},{16,12},{20,16},{24,20},{28,24},{32,28},{36,32}... | collective-permute-start | bytes 98312 | tf_op jit(solution)/shard_map/ppermute | solution.py:688
  192.3 5.3 %collective-permute-done.3.borrowed_ref = f32[32,256]{1,0:T(8,128)S(1)} collective-permute-done((f32[32,256]{1,0:T(8,128)}, f32[32,256]{1,0:T(8,128)S(1)}, u32[]{:S(2)}, u32[]{:S(2)}) %collective-permute-start.3) | collective-permute-done | bytes 32800 | tf_op jit(solution)/shard_map/ppermute | solution.py:688
  197.6 0.6 copy-done.5
  198.2 0.1 copy-done.3
  198.3 21.5 %own.1 = f32[4096,256]{1,0:T(8,128)} custom-call(s32[264]{0:T(512)} %get-tuple-element.35.order_ref, s32[3]{0:T(128)} %get-tuple-element.36.bounds_ref, s32[256]{0:T(256)} %get-tuple-element.37.wanted_ref, bf16[256,128,256]{2,1,0:T(8,128)(2,1)} %recompute.2.ctx_ref, bf16[128,128,256]{2,1,0:T(8,128)(2,1)} %collective-permute-done.2.help_ref, ...), custom_call_target="tpu_custom_call" | custom-call | tf_op jit(solution)/shard_map/own/pallas_call | solution.py:653
  (16 shorter events, 0.1 us)
Async XLA Ops:
  1.5 4.4 %collective-permute-start = (bf16[8,128]{1,0:T(8,128)(2,1)S(1)}, bf16[8,128]{1,0:T(8,128)(2,1)S(1)}, u32[]{:S(2)}, u32[]{:S(2)}) collective-permute-start(bf16[8,128]{1,0:T(8,128)(2,1)S(1)} %pad_maximum_fusion), channel_id=1, source_target_pairs={{0,4},{4,8},{8,12},{12,16},{16,20},{20,24},{24,28},{28,32},{32,36}... | collective-permute-start | bytes 6152 | tf_op jit(solution)/shard_map/ppermute | solution.py:688
  5.9 0.5 copy-start.6
  11.9 11.2 %copy-start.1 = (bf16[4,2,256,256]{3,2,1,0:T(8,128)(2,1)S(1)}, bf16[4,2,256,256]{3,2,1,0:T(8,128)(2,1)}, u32[]{:S(2)}) copy-start(bf16[4,2,256,256]{3,2,1,0:T(8,128)(2,1)} %param.12) | copy-start | bytes 3145732
  11.9 38.2 %all-to-all-start = ((bf16[128,2,32,128]{3,2,1,0:T(8,128)(2,1)}), bf16[128,2,32,128]{3,2,1,0:T(8,128)(2,1)S(1)}, u32[]{:S(2)}, u32[]{:S(2)}) async-start(bf16[128,2,32,128]{3,2,1,0:T(8,128)(2,1)} %bitcast.25), calls=%async_computation | async-start | bytes 4194304 | tf_op jit(solution)/shard_map/all_to_all | solution.py:698
  50.1 1.3 copy-start
  57.7 3.0 %collective-permute-start.1 = (bf16[129,32,128]{2,1,0:T(8,128)(2,1)}, bf16[129,32,128]{2,1,0:T(8,128)(2,1)S(1)}, u32[]{:S(2)}, u32[]{:S(2)}) collective-permute-start(bf16[129,32,128]{2,1,0:T(8,128)(2,1)} %get-tuple-element.40), channel_id=1, source_target_pairs={{0,4},{4,0},{8,12},{12,8},{16,20},{20,16},{24,28},{28,24},{32,36},... | collective-permute-start | bytes 3170312 | tf_op jit(solution)/shard_map/ppermute | solution.py:692
  60.7 2.3 %copy-start.7 = (bf16[129,32,128]{2,1,0:T(8,128)(2,1)}, bf16[129,32,128]{2,1,0:T(8,128)(2,1)S(1)}, u32[]{:S(2)}) copy-start(bf16[129,32,128]{2,1,0:T(8,128)(2,1)S(1)} %collective-permute-done.1.push_ref) | copy-start | bytes 3170308
  66.4 17.5 %copy-start.4 = (bf16[256,256]{1,0:T(8,128)(2,1)S(1)}, bf16[256,256]{1,0:T(8,128)(2,1)}, u32[]{:S(2)}) copy-start(bf16[256,256]{1,0:T(8,128)(2,1)} %pred_ref.5) | copy-start | bytes 393220
  66.4 131.2 %collective-permute-start.2 = (bf16[128,128,256]{2,1,0:T(8,128)(2,1)}, bf16[128,128,256]{2,1,0:T(8,128)(2,1)}, u32[]{:S(2)}, u32[]{:S(2)}) collective-permute-start(bf16[128,128,256]{2,1,0:T(8,128)(2,1)} %recompute.3), channel_id=1, source_target_pairs={{0,4},{4,0},{8,12},{12,8},{16,20},{20,16},{24,28},{28,24},{32,36},... | collective-permute-start | bytes 25165832 | tf_op jit(solution)/shard_map/ppermute | solution.py:692
  84.6 58.2 %all-to-all-start.1 = ((bf16[128,2,32,128]{3,2,1,0:T(8,128)(2,1)}), bf16[128,2,32,128]{3,2,1,0:T(8,128)(2,1)S(1)}, u32[]{:S(2)}, u32[]{:S(2)}) async-start(bf16[128,2,32,128]{3,2,1,0:T(8,128)(2,1)} %bitcast.8), calls=%async_computation.1 | async-start | bytes 4194304 | tf_op jit(solution)/shard_map/all_to_all | solution.py:698
  142.8 1.3 copy-start.2
  164.6 33.0 %all-to-all-start.2 = ((f32[128,2,2,128]{3,2,1,0:T(2,128)}), f32[128,2,2,128]{3,2,1,0:T(2,128)S(1)}, u32[]{:S(2)}, u32[]{:S(2)}) async-start(f32[128,2,2,128]{3,2,1,0:T(2,128)} %bitcast.30), calls=%async_computation.2 | async-start | bytes 524288 | tf_op jit(solution)/shard_map/all_to_all | solution.py:698
  190.0 7.5 %collective-permute-start.3 = (f32[32,256]{1,0:T(8,128)}, f32[32,256]{1,0:T(8,128)S(1)}, u32[]{:S(2)}, u32[]{:S(2)}) collective-permute-start(f32[32,256]{1,0:T(8,128)} %get-tuple-element.54), channel_id=1, source_target_pairs={{4,0},{8,4},{12,8},{16,12},{20,16},{24,20},{28,24},{32,28},{36,32}... | collective-permute-start | bytes 98312 | tf_op jit(solution)/shard_map/ppermute | solution.py:688
  197.6 0.6 copy-start.5
  197.6 0.7 copy-start.3
